TPU v7x, 256 devices: a whole 4x4x8 slice. The times are simulated.
256 devices in a mesh: slide: 32 (over x, y, core), tile: 8 (over z).
Axes of the slice: x: 4, y: 4, z: 8, core: 2. Of those that a mesh axis runs over, the one named last changes fastest.
Arguments:
- image: bfloat16 [32, 3, 64, 2048], P('slide', None, 'tile'), may hold values from -6 to 6
- stem_weight: bfloat16 [147, 64], replicated, may hold values from -0.5 to 0.5
- conv_weight: bfloat16 [576, 64], replicated, may hold values from -0.25 to 0.25
- expand_weight: bfloat16 [64, 256], replicated, may hold values from -0.75 to 0.75
- cotangent: bfloat16 [32, 32, 262144], P('slide', 'tile'), may hold values from -6 to 6
- tissue: int32 [32, 1, 4], P('slide'), may hold values 0 or 1
Outputs:
- stem_grad: bfloat16 [32, 32, 65536], P('slide', 'tile')
- stem_wgrad: float32 [147, 64], replicated
- conv_wgrad: float32 [576, 64], replicated
- expand_wgrad: float32 [64, 256], replicated
All inputs are finite; a program needn't handle non-finite values. No bound on the sum of `tissue` on one device may be relied on, other than what follows from the above.
Results may differ from a plain program's by a relative error of at most 0.0055.
Values may be sent and summed in bfloat16 or wider, within the bound.
No kernel may reach another device: no remote copies, remote signals or barrier semaphores. Data moves between devices by JAX's collectives and lax.ppermute only.
A program may use at most 64 MiB of HBM per device.

v0:
```python
import jax
import jax.numpy as jnp
from jax import lax
from jax.experimental import pallas as pl
from jax.experimental.layout import Layout, with_layout_constraint
from jax.experimental.pallas import tpu as pltpu
from jax.sharding import Mesh, PartitionSpec as P

F32 = jnp.float32
BF16 = jnp.bfloat16
VMEM_LIMIT = 56 * 1024 * 1024

ROW_OF = (1, 2, 3, 4, 0, 5)
SLOT_OF = (4, 0, 1, 2, 3, 5)
PAD = 8


def dot_t(left, right):
    return lax.dot_general(left, right, (((1,), (1,)), ((), ())), preferred_element_type=F32)


def dot_0(left, right):
    return lax.dot_general(left, right, (((0,), (0,)), ((), ())), preferred_element_type=F32)


def dot_n(left, right):
    return jnp.dot(left, right, preferred_element_type=F32)


def iota(shape, dim):
    return lax.broadcasted_iota(jnp.int32, shape, dim)


def lane_is_low(rows):
    return iota((rows, 128), 1) < 64


def stem_places(row, count, split):
    lane = iota((1, 512), 1)
    tap = lane // 64
    within = lane % 64
    colour = (within >= 18).astype(jnp.int32) + (within >= 36).astype(jnp.int32)
    line = within - 18 * colour - 2 * row
    valid = (tap >= 1) & (within < 54) & (line >= 0) & (line <= 6)
    entry = line * 21 + (tap - 1) * 3 + colour
    if split:
        entry = jnp.where(entry < 128, entry, entry + 64)
    entry = jnp.where(valid, entry, -1)
    return (iota((count, 512), 0) == entry).astype(F32).astype(BF16)


def prepare_kernel(tissue, cot, stem_t, conv_t, expand, cot_f, back2, w1, w2, w2b, order, wide):
    step = pl.program_id(0)

    @pl.when(step == 0)
    def _():
        m, k = iota((256, 256), 0), iota((256, 256), 1)
        source = (m % 32) * 8 + ((m // 32) % 2) * 4 + m // 64
        order[...] = (k == source).astype(F32).astype(BF16)
        wide[...] = jnp.zeros(wide.shape, BF16)
        for r in range(4):
            wide[r * 64 : (r + 1) * 64, r * 256 : (r + 1) * 256] = expand[...]
        stem = stem_t[...]
        for slot in range(6):
            w1[slot * 64 : (slot + 1) * 64, :] = dot_n(stem, stem_places(ROW_OF[slot], 256, False)).astype(BF16)
        blocks = [conv_t[:, n * 64 : (n + 1) * 64].astype(F32) for n in range(9)]
        none = jnp.zeros((64, 64), F32)

        def block(i, j):
            return blocks[3 * i + j] if 0 <= i <= 2 else none

        for j in range(3):
            for r in range(4):
                for t in range(3):
                    pair = [block(ROW_OF[2 * t + e] - r, j) for e in range(2)]
                    w2[r * 64 : (r + 1) * 64, j * 384 + t * 128 : j * 384 + (t + 1) * 128] = jnp.concatenate(pair, 1).astype(BF16)
            for slot in range(6):
                for t in range(2):
                    pair = [block(2 * t + e - ROW_OF[slot] + 2, j) for e in range(2)]
                    w2b[slot * 64 : (slot + 1) * 64, j * 256 + t * 128 : j * 256 + (t + 1) * 128] = jnp.concatenate(pair, 1).astype(BF16)

    for s in range(8):
        got = dot_n(order[...], cot[s * 256 : (s + 1) * 256, :]).astype(BF16)
        for n in range(8):
            cot_f[s * 32 : (s + 1) * 32, n * 128 : (n + 1) * 128] = got[n * 32 : (n + 1) * 32, :]
    keep = tissue[0, step].astype(F32)
    back2[...] = dot_t(cot_f[...], wide[...]) * keep


def forward_kernel(tissue, place, before, own, after, w1, w2, back2, z, act_sh, slope1, act2, grad2, edge, lines, cols, field):
    lines[54:64, :] = jnp.zeros((10, 2048), F32)
    for k in range(3):
        lines[18 * k : 18 * k + 5, :] = before[0, k, 3:8, :].astype(F32)
        lines[18 * k + 5 : 18 * k + 13, :] = own[0, k].astype(F32)
        lines[18 * k + 13 : 18 * k + 18, :] = after[0, k, 0:5, :].astype(F32)
    m, x = iota((128, 512), 0), iota((128, 512), 1)
    pick = (x == jnp.where(x < 256, 2 * m, 2 * m + 257)).astype(F32).astype(BF16)
    cols[0:PAD, :] = jnp.zeros((PAD, 128), F32)
    cols[PAD + 1024 :, :] = jnp.zeros((PAD, 128), F32)
    field[0:PAD, :] = jnp.zeros((PAD, 384), F32)
    field[PAD + 1024 :, :] = jnp.zeros((PAD, 384), F32)
    none = jnp.zeros((64, 256), BF16)
    for t in range(8):
        part = lines[:, t * 256 : (t + 1) * 256].astype(BF16)
        spread = jnp.concatenate([jnp.concatenate([part, none], 0), jnp.concatenate([none, part], 0)], 1)
        cols[PAD + t * 128 : PAD + (t + 1) * 128, :] = dot_t(pick, spread)
    above, below = place[0, 0].astype(F32), place[0, 1].astype(F32)
    ends = jnp.where(lane_is_low(1), above, below)
    for t in range(8):
        at = t * 128
        wins = [cols[PAD + at + s : PAD + at + s + 128, :].astype(BF16) for s in (-2, -1, 0, 1)]
        zt = jnp.concatenate(wins, 1)
        z[at : at + 128, :] = zt
        pre = dot_t(zt, w1[...])
        sig = 1.0 / (1.0 + jnp.exp(-pre))
        act = pre * sig
        field[PAD + at : PAD + at + 128, 0:256] = act[:, :256]
        field[PAD + at : PAD + at + 128, 256:384] = act[:, 256:] * ends
        slope1[at : at + 128, :] = (sig * (1.0 + pre * (1.0 - sig)))[:, :256]
    for t in range(8):
        at = t * 128
        wins = [field[PAD + at + j - 1 : PAD + at + j + 127, :].astype(BF16) for j in range(3)]
        sh = jnp.concatenate(wins, 1)
        act_sh[at : at + 128, :] = sh
        pre = dot_t(sh, w2[...])
        sig = 1.0 / (1.0 + jnp.exp(-pre))
        keep = tissue[0, t // 2].astype(F32)
        act2[at : at + 128, :] = (pre * sig * keep).astype(BF16)
        slope = sig * (1.0 + pre * (1.0 - sig))
        grad2[at : at + 128, :] = (back2[at : at + 128, :] * slope).astype(BF16)
    low = lane_is_low(512)
    a, b = grad2[0:512, 0:128].astype(F32), grad2[512:1024, 0:128].astype(F32)
    edge[0] = jnp.where(low, a, pltpu.roll(b, 64, 1)).astype(BF16)
    a, b = grad2[0:512, 128:256].astype(F32), grad2[512:1024, 128:256].astype(F32)
    edge[1] = jnp.where(low, pltpu.roll(a, 64, 1), b).astype(BF16)


def filters_kernel(act_sh, act2, grad2, cot_f, sums):
    prod = dot_0(grad2[...], act_sh[...])
    low = lane_is_low(64)
    halves = {}
    for i in range(3):
        for j in range(3):
            at_low, at_high = [], []
            for r in range(4):
                slot = SLOT_OF[r + i]
                col = j * 384 + (slot // 2) * 128
                tile = prod[r * 64 : (r + 1) * 64, col : col + 128]
                (at_high if slot % 2 else at_low).append(tile)
            halves[3 * i + j] = (sum(at_low[1:], at_low[0]), sum(at_high[1:], at_high[0]))
    for u in range(5):
        a, b = halves[2 * u]
        left = a + pltpu.roll(b, 64, 1)
        if u == 4:
            tile = jnp.where(low, left, 0.0)
        else:
            a, b = halves[2 * u + 1]
            tile = jnp.where(low, left, pltpu.roll(a, 64, 1) + b)
        sums[u * 64 : (u + 1) * 64, :] = tile
    total = None
    for t in range(2):
        pair = dot_0(act2[:, t * 128 : (t + 1) * 128], cot_f[:, t * 512 : (t + 1) * 512])
        part = pair[0:64, 0:256] + pair[64:128, 256:512]
        total = part if total is None else total + part
    sums[320:384, :] = total[:, 0:128]
    sums[384:448, :] = total[:, 128:256]


def backward_kernel(z, slope1, grad2, halo_a, halo_b, w2b, sums, out, totals, wide, mixed):
    low = lane_is_low(512)
    a, b = halo_a[...].astype(F32), halo_b[...].astype(F32)
    ends = [jnp.where(low, a, pltpu.roll(b, 64, 1)).astype(BF16), jnp.where(low, pltpu.roll(a, 64, 1), b).astype(BF16)]
    wide[0:PAD, :] = jnp.zeros((PAD, 768), F32)
    wide[PAD + 1024 :, :] = jnp.zeros((PAD, 768), F32)
    for t in range(8):
        at = t * 128
        end = ends[t // 4][(t % 4) * 128 : (t % 4 + 1) * 128, :]
        left = jnp.concatenate([grad2[at : at + 128, :], end], 1)
        wide[PAD + at : PAD + at + 128, :] = dot_n(left, w2b[...])
    for t in range(8):
        at = t * 128
        back = wide[PAD + at + 1 : PAD + at + 129, 0:256] + wide[PAD + at : PAD + at + 128, 256:512]
        back = back + wide[PAD + at - 1 : PAD + at + 127, 512:768]
        grad = back * slope1[at : at + 128, :]
        gb = grad.astype(BF16)
        mixed[0, at : at + 128, :] = gb
        gr = gb.astype(F32)
        turned = [pltpu.roll(gr[:, u * 128 : (u + 1) * 128], 64, 1) for u in range(2)]
        mixed[1, at : at + 128, :] = jnp.concatenate(turned, 1).astype(BF16)
    n, k = iota((256, 256), 0), iota((256, 256), 1)
    odd, r, pair = n // 128, n % 4, (n % 128) // 4
    source = (r // 2) * 128 + ((r + odd) % 2) * 64 + 2 * pair + odd
    order = (k == source).astype(F32).astype(BF16)
    low = lane_is_low(128)
    for t in range(16):
        at = t * 64
        stack = jnp.concatenate(
            [mixed[v, at : at + 64, u * 128 : (u + 1) * 128] for u in range(2) for v in range(2)], 0
        )
        got = dot_n(order, stack)
        out[t * 128 : (t + 1) * 128, :] = jnp.where(low, got[0:128], got[128:256]).astype(BF16)
    prod = dot_0(mixed[0], z[...])
    stem = None
    for r in range(4):
        part = prod[r * 64 : (r + 1) * 64, :]
        places = stem_places(r + 1, 256, True)
        for _ in range(3):
            piece = part.astype(BF16)
            term = dot_t(piece, places)
            stem = term if stem is None else stem + term
            part = part - piece.astype(F32)
    totals[0:448, :] = sums[...]
    totals[256:320, :] = jnp.where(lane_is_low(64), sums[256:320, :], stem[:, 128:256])
    totals[448:512, :] = stem[:, 0:128]


def unpack_kernel(totals, factor, stem_t, conv_t, expand):
    scale = factor[0, 0]
    for u in range(4):
        conv_t[:, u * 128 : (u + 1) * 128] = totals[u * 64 : (u + 1) * 64, :] * scale
    mixed = totals[256:320, :] * scale
    conv_t[:, 512:576] = mixed[:, 0:64]
    stem_t[:, 0:128] = totals[448:512, :] * scale
    stem_t[:, 128:147] = pltpu.roll(mixed, 64, 1)[:, 0:19]
    for u in range(2):
        expand[:, u * 128 : (u + 1) * 128] = totals[320 + u * 64 : 384 + u * 64, :] * scale


def params():
    return pltpu.CompilerParams(vmem_limit_bytes=VMEM_LIMIT)


def shapes(*pairs):
    return [jax.ShapeDtypeStruct(shape, dtype) for shape, dtype in pairs]


SMEM = pl.BlockSpec(memory_space=pltpu.SMEM)
WHOLE = pl.BlockSpec(memory_space=pltpu.VMEM)


def prepare(tissue, cot, stem_t, conv_t, expand):
    def fixed(shape):
        return pl.BlockSpec(shape, lambda i: (0, 0))

    return pl.pallas_call(
        prepare_kernel,
        grid=(4,),
        in_specs=[SMEM, pl.BlockSpec((2048, 128), lambda i: (i, 0)), fixed((64, 256)), fixed((64, 576)), fixed((64, 256))],
        out_specs=[
            pl.BlockSpec((256, 1024), lambda i: (i, 0)),
            pl.BlockSpec((256, 256), lambda i: (i, 0)),
            fixed((384, 512)),
            fixed((256, 1152)),
            fixed((384, 768)),
        ],
        out_shape=shapes(((1024, 1024), BF16), ((1024, 256), F32), ((384, 512), BF16), ((256, 1152), BF16), ((384, 768), BF16)),
        scratch_shapes=[pltpu.VMEM((256, 256), BF16), pltpu.VMEM((256, 1024), BF16)],
        compiler_params=params(),
        name="prepare",
    )(tissue, cot, stem_t, conv_t, expand)


def forward(tissue, place, before, own, after, w1, w2, back2):
    return pl.pallas_call(
        forward_kernel,
        in_specs=[SMEM, SMEM] + [WHOLE] * 6,
        out_specs=[WHOLE] * 6,
        out_shape=shapes(
            ((1024, 512), BF16), ((1024, 1152), BF16), ((1024, 256), F32), ((1024, 256), BF16), ((1024, 256), BF16), ((2, 512, 128), BF16)
        ),
        scratch_shapes=[pltpu.VMEM((64, 2048), F32), pltpu.VMEM((1024 + 2 * PAD, 128), F32), pltpu.VMEM((1024 + 2 * PAD, 384), F32)],
        compiler_params=params(),
        name="forward",
    )(tissue, place, before, own, after, w1, w2, back2)


def filters(act_sh, act2, grad2, cot_f):
    return pl.pallas_call(
        filters_kernel,
        in_specs=[WHOLE] * 4,
        out_specs=WHOLE,
        out_shape=jax.ShapeDtypeStruct((448, 128), F32),
        compiler_params=params(),
        name="filters",
    )(act_sh, act2, grad2, cot_f)


def backward(z, slope1, grad2, halo_a, halo_b, w2b, sums):
    return pl.pallas_call(
        backward_kernel,
        in_specs=[WHOLE] * 7,
        out_specs=[WHOLE] * 2,
        out_shape=shapes(((2048, 128), BF16), ((512, 128), F32)),
        scratch_shapes=[pltpu.VMEM((1024 + 2 * PAD, 768), F32), pltpu.VMEM((2, 1024, 256), BF16)],
        compiler_params=params(),
        name="backward",
    )(z, slope1, grad2, halo_a, halo_b, w2b, sums)


def unpack(totals, factor):
    return pl.pallas_call(
        unpack_kernel,
        in_specs=[WHOLE, SMEM],
        out_specs=[WHOLE] * 3,
        out_shape=shapes(((64, 147), F32), ((64, 576), F32), ((64, 256), F32)),
        compiler_params=params(),
        name="unpack",
    )(totals, factor)


def reduce_all(totals):
    slide = ("x", "y", "core")
    count, depth = lax.axis_size(slide), lax.axis_size("tile")
    part = lax.all_to_all(totals.reshape(count, -1, 128), slide, 0, 0, tiled=True).sum(0)
    part = lax.all_to_all(jnp.broadcast_to(part[None], (depth,) + part.shape), "tile", 0, 0, tiled=True).sum(0)
    whole = lax.all_to_all(jnp.broadcast_to(part[None], (count,) + part.shape), slide, 0, 0, tiled=True)
    return whole.reshape(totals.shape)


def per_device(image, stem_weight, conv_weight, expand_weight, cotangent, tissue):
    depth = lax.axis_size("tile")
    position = lax.axis_index("tile")
    down = [(i, i + 1) for i in range(depth - 1)]
    up = [(i + 1, i) for i in range(depth - 1)]
    before = lax.ppermute(image, "tile", down)
    after = lax.ppermute(image, "tile", up)
    place = jnp.stack([position > 0, position < depth - 1]).astype(jnp.int32)[None]
    rows = tissue[0]
    cot = cotangent[0].reshape(4, 1024, 2, 128).transpose(1, 2, 0, 3).reshape(8192, 128)
    stem_t = jnp.pad(stem_weight.T, ((0, 0), (0, 109)))
    cot_f, back2, w1, w2, w2b = prepare(rows, cot, stem_t, conv_weight.T, expand_weight)
    z, act_sh, slope1, act2, grad2, edge = forward(rows, place, before, image, after, w1, w2, back2)
    halo_b = lax.ppermute(edge[0], "tile", up)
    halo_a = lax.ppermute(edge[1], "tile", down)
    sums = filters(act_sh, act2, grad2, cot_f)
    out, totals = backward(z, slope1, grad2, halo_a, halo_b, w2b, sums)
    totals = reduce_all(totals)
    factor = jnp.full((1, 1), 1.0 / 1024.0, F32)
    stem_g, conv_g, expand_g = unpack(totals, factor)
    field = out.reshape(512, 4, 128).transpose(1, 0, 2)
    field = with_layout_constraint(field, Layout(major_to_minor=(1, 0, 2)))
    return field.reshape(1, 4, 65536), stem_g.T, conv_g.T, expand_g


def solution(mesh):
    slide = ("x", "y", "core")
    fine = Mesh(mesh.devices.reshape(4, 4, 2, 8), slide + ("tile",))
    placed = (P(slide, None, "tile", None), P(), P(), P(), P(slide, "tile", None), P(slide, None, None))
    return jax.shard_map(
        per_device, mesh=fine, in_specs=placed, out_specs=(P(slide, "tile", None), P(), P(), P()), check_vma=False
    )
```

profile of v0, /device:TPU:1, one launch (start us, length us, event | category | flops | bytes accessed | tf_op | source)
XLA Modules:
  0.0 91.6 jit_solution(3423459679940942190)
XLA Ops:
  0.6 4.4 %collective-permute-start = (bf16[1,3,8,2048]{3,2,1,0:T(8,128)(2,1)}, bf16[1,3,8,2048]{3,2,1,0:T(8,128)(2,1)S(1)}, u32[]{:S(2)}, u32[]{:S(2)}) collective-permute-start(bf16[1,3,8,2048]{3,2,1,0:T(8,128)(2,1)} %own.1), channel_id=1, source_target_pairs={{0,1},{1,2},{2,3},{3,4},{4,5},{5,6},{6,7},{8,9},{9,10},{10,11},{11... | collective-permute-start | bytes 294920 | tf_op jit(solution)/shard_map/ppermute | solution.py:325
  5.0 1.3 %collective-permute-start.1 = (bf16[1,3,8,2048]{3,2,1,0:T(8,128)(2,1)}, bf16[1,3,8,2048]{3,2,1,0:T(8,128)(2,1)S(1)}, u32[]{:S(2)}, u32[]{:S(2)}) collective-permute-start(bf16[1,3,8,2048]{3,2,1,0:T(8,128)(2,1)} %own.1), channel_id=1, source_target_pairs={{1,0},{2,1},{3,2},{4,3},{5,4},{6,5},{7,6},{9,8},{10,9},{11,10},{12... | collective-permute-start | bytes 294920 | tf_op jit(solution)/shard_map/ppermute | solution.py:326
  6.3 1.4 %pad.4.stem_t = bf16[64,256]{1,0:T(8,128)(2,1)} pad(bf16[64,147]{1,0:T(8,128)(2,1)} %bitcast.27, bf16[]{:T(256)} %constant.5.clone.1), padding=0_0x0_109 | pad | bytes 51586 | tf_op jit(solution)/shard_map/jit(_pad)/pad | solution.py:330
  7.7 6.4 %prepare.1 = (bf16[1024,1024]{1,0:T(8,128)(2,1)}, f32[1024,256]{1,0:T(8,128)}, bf16[384,512]{1,0:T(8,128)(2,1)}, bf16[256,1152]{1,0:T(8,128)(2,1)}, bf16[384,768]{1,0:T(8,128)(2,1)}) custom-call(s32[1,4]{1,0:T(1,128)} %bitcast.28, bf16[8192,128]{1,0:T(8,128)(2,1)} %bitcast.23, bf16[64,256]{1,0:T(8,128)(2,1)} %pad.4.stem_t, bf16[64,576]{1,0:T(8,128)(2,1)} %bitcast.26, ...), custom_call_target="tpu_custom_call" | custom-call | tf_op jit(solution)/shard_map/prepare/pallas_call | solution.py:245
  14.1 0.6 add_convert_fusion.place
  14.7 0.0 collective-permute-done.before
  14.7 0.0 copy-start.2
  14.7 0.0 collective-permute-done.1.after
  14.7 0.0 copy-start.3
  14.7 0.6 copy-done.2
  15.3 0.0 copy-done.3
  15.3 7.1 %forward.1 = (bf16[1024,512]{1,0:T(8,128)(2,1)}, bf16[1024,1152]{1,0:T(8,128)(2,1)}, f32[1024,256]{1,0:T(8,128)}, bf16[1024,256]{1,0:T(8,128)(2,1)}, bf16[1024,2...) custom-call(s32[1,4]{1,0:T(1,128)} %bitcast.29, s32[1,2]{1,0:T(1,128)} %add_convert_fusion.place, ...), custom_call_target="tpu_custom_call" | custom-call | tf_op jit(solution)/shard_map/forward/pallas_call | solution.py:264
  22.5 1.0 %slice_bitcast_fusion = (bf16[512,128]{1,0:T(8,128)(2,1)S(1)}, bf16[512,128]{1,0:T(8,128)(2,1)S(1)}) fusion(bf16[2,512,128]{2,1,0:T(8,128)(2,1)} %get-tuple-element.26), kind=kLoop, calls=%fused_computation | loop fusion | bytes 524288 | tf_op jit(solution)/shard_map/squeeze | solution.py:333
  23.4 1.3 %collective-permute-start.3 = (bf16[512,128]{1,0:T(8,128)(2,1)S(1)}, bf16[512,128]{1,0:T(8,128)(2,1)S(1)}, u32[]{:S(2)}, u32[]{:S(2)}) collective-permute-start(bf16[512,128]{1,0:T(8,128)(2,1)S(1)} %get-tuple-element.36), channel_id=1, source_target_pairs={{1,0},{2,1},{3,2},{4,3},{5,4},{6,5},{7,6},{9,8},{10,9},{11,10},{12... | collective-permute-start | bytes 393224 | tf_op jit(solution)/shard_map/ppermute | solution.py:333
  24.7 4.8 %collective-permute-start.2 = (bf16[512,128]{1,0:T(8,128)(2,1)S(1)}, bf16[512,128]{1,0:T(8,128)(2,1)S(1)}, u32[]{:S(2)}, u32[]{:S(2)}) collective-permute-start(bf16[512,128]{1,0:T(8,128)(2,1)S(1)} %get-tuple-element.37), channel_id=1, source_target_pairs={{0,1},{1,2},{2,3},{3,4},{4,5},{5,6},{6,7},{8,9},{9,10},{10,11},{11... | collective-permute-start | bytes 393224 | tf_op jit(solution)/shard_map/ppermute | solution.py:334
  29.6 4.6 %filters.1.sums = f32[448,128]{1,0:T(8,128)} custom-call(bf16[1024,1152]{1,0:T(8,128)(2,1)} %get-tuple-element.28.act_sh, bf16[1024,256]{1,0:T(8,128)(2,1)} %get-tuple-element.29.act2, bf16[1024,256]{1,0:T(8,128)(2,1)} %get-tuple-element.25.grad2, bf16[1024,1024]{1,0:T(8,128)(2,1)} %get-tuple-element.30.cot_f), custom_call_target="tpu_custom_call" | custom-call | tf_op jit(solution)/shard_map/filters/pallas_call | solution.py:278
  34.1 0.0 collective-permute-done.3.halo_b
  34.1 0.0 copy-start
  34.1 0.0 collective-permute-done.2.halo_a
  34.1 0.0 copy-start.1
  34.2 0.6 copy-done
  34.8 0.0 copy-done.1
  34.8 7.0 %backward.1 = (bf16[2048,128]{1,0:T(8,128)(2,1)}, f32[512,128]{1,0:T(8,128)}) custom-call(bf16[1024,512]{1,0:T(8,128)(2,1)} %get-tuple-element.23.z, f32[1024,256]{1,0:T(8,128)} %get-tuple-element.24.slope1, bf16[1024,256]{1,0:T(8,128)(2,1)} %get-tuple-element.25.grad2, bf16[512,128]{1,0:T(8,128)(2,1)} %copy-done.1, bf16[512,128]{1,0:T(8,128)(2,1)} %copy-done, ...), custom_call_target="tpu_custom_call" | custom-call | tf_op jit(solution)/shard_map/backward/pallas_call | solution.py:289
  41.9 17.4 %all_to_all.15 = f32[32,16,128]{2,1,0:T(8,128)S(1)} all-to-all(f32[32,16,128]{2,1,0:T(8,128)} %bitcast.25), channel_id=1, replica_groups=mesh['x'=4,'y'=4,'core'=2,'tile'=8] {'x','y','core'}, dimensions={0} | all-to-all | bytes 524288 | tf_op jit(solution)/shard_map/all_to_all | solution.py:314
  59.3 16.5 %all_to_all.16 = f32[8,16,128]{2,1,0:T(8,128)S(1)} all-to-all(f32[8,16,128]{2,1,0:T(8,128)S(1)} %broadcast_in_dim.4), channel_id=1, replica_groups=mesh['x'=4,'y'=4,'core'=2,'tile'=8] {'tile'}, dimensions={0} | all-to-all | bytes 131072 | tf_op jit(solution)/shard_map/all_to_all | solution.py:315
  75.8 14.1 %all_to_all.17 = f32[32,16,128]{2,1,0:T(8,128)} all-to-all(f32[32,16,128]{2,1,0:T(8,128)S(1)} %broadcast_in_dim.5), channel_id=1, replica_groups=mesh['x'=4,'y'=4,'core'=2,'tile'=8] {'x','y','core'}, dimensions={0} | all-to-all | bytes 524288 | tf_op jit(solution)/shard_map/all_to_all | solution.py:316
  89.9 1.7 %unpack.1 = (f32[64,147]{1,0:T(8,128)}, f32[64,576]{1,0:T(8,128)}, f32[64,256]{1,0:T(8,128)}) custom-call(f32[512,128]{1,0:T(8,128)} %bitcast.24, f32[1,1]{1,0:T(1,128)} %constant.13.clone.1.factor), custom_call_target="tpu_custom_call" | custom-call | tf_op jit(solution)/shard_map/unpack/pallas_call | solution.py:301
  (4 shorter events, 0.1 us)
Async XLA Ops:
  0.6 14.1 %collective-permute-start = (bf16[1,3,8,2048]{3,2,1,0:T(8,128)(2,1)}, bf16[1,3,8,2048]{3,2,1,0:T(8,128)(2,1)S(1)}, u32[]{:S(2)}, u32[]{:S(2)}) collective-permute-start(bf16[1,3,8,2048]{3,2,1,0:T(8,128)(2,1)} %own.1), channel_id=1, source_target_pairs={{0,1},{1,2},{2,3},{3,4},{4,5},{5,6},{6,7},{8,9},{9,10},{10,11},{11... | collective-permute-start | bytes 294920 | tf_op jit(solution)/shard_map/ppermute | solution.py:325
  5.0 9.7 %collective-permute-start.1 = (bf16[1,3,8,2048]{3,2,1,0:T(8,128)(2,1)}, bf16[1,3,8,2048]{3,2,1,0:T(8,128)(2,1)S(1)}, u32[]{:S(2)}, u32[]{:S(2)}) collective-permute-start(bf16[1,3,8,2048]{3,2,1,0:T(8,128)(2,1)} %own.1), channel_id=1, source_target_pairs={{1,0},{2,1},{3,2},{4,3},{5,4},{6,5},{7,6},{9,8},{10,9},{11,10},{12... | collective-permute-start | bytes 294920 | tf_op jit(solution)/shard_map/ppermute | solution.py:326
  14.7 0.6 copy-start.2
  14.7 0.7 copy-start.3
  23.4 10.7 %collective-permute-start.3 = (bf16[512,128]{1,0:T(8,128)(2,1)S(1)}, bf16[512,128]{1,0:T(8,128)(2,1)S(1)}, u32[]{:S(2)}, u32[]{:S(2)}) collective-permute-start(bf16[512,128]{1,0:T(8,128)(2,1)S(1)} %get-tuple-element.36), channel_id=1, source_target_pairs={{1,0},{2,1},{3,2},{4,3},{5,4},{6,5},{7,6},{9,8},{10,9},{11,10},{12... | collective-permute-start | bytes 393224 | tf_op jit(solution)/shard_map/ppermute | solution.py:333
  24.7 9.4 %collective-permute-start.2 = (bf16[512,128]{1,0:T(8,128)(2,1)S(1)}, bf16[512,128]{1,0:T(8,128)(2,1)S(1)}, u32[]{:S(2)}, u32[]{:S(2)}) collective-permute-start(bf16[512,128]{1,0:T(8,128)(2,1)S(1)} %get-tuple-element.37), channel_id=1, source_target_pairs={{0,1},{1,2},{2,3},{3,4},{4,5},{5,6},{6,7},{8,9},{9,10},{10,11},{11... | collective-permute-start | bytes 393224 | tf_op jit(solution)/shard_map/ppermute | solution.py:334
  34.1 0.7 copy-start
  34.1 0.7 copy-start.1
where the time goes:
time: 92.2 us; the launch traced here: 91.6 us
  blocking collectives  47.9 us (52%)
  Pallas kernels  26.8 us (29%)
  starting transfers between devices  11.8 us (13%)
  local copies, waits for them, and re-layouts  3.72 us (4%)
    all_to_all x1, blocking collectives, reduce_all(): lax.all_to_all(totals.reshape(count, -1, 128), slide, 0, 0, tiled=True)  17.4 us
    all_to_all x1, blocking collectives, reduce_all(): lax.all_to_all(jnp.broadcast_to(part[None], (depth,) + part.shape), 'tile...  16.5 us
    all_to_all x1, blocking collectives, reduce_all(): lax.all_to_all(jnp.broadcast_to(part[None], (count,) + part.shape), slide...  14.1 us
    pallas_call x1, Pallas kernels, forward(): pl.pallas_call(forward_kernel, in_specs=[SMEM, SMEM] + [WHOLE] * 6, out_s...  7.11 us
    pallas_call x1, Pallas kernels, backward(): pl.pallas_call(backward_kernel, in_specs=[WHOLE] * 7, out_specs=[WHOLE] *...  7.05 us
    pallas_call x1, Pallas kernels, prepare(): pl.pallas_call(prepare_kernel, grid=(4,), in_specs=[SMEM, pl.BlockSpec((2...  6.39 us
    ppermute x1, starting transfers between devices, per_device(): halo_a = lax.ppermute(edge[1], 'tile', down)  4.81 us
    pallas_call x1, Pallas kernels, filters(): pl.pallas_call(filters_kernel, in_specs=[WHOLE] * 4, out_specs=WHOLE, out...  4.57 us
  transfers between devices with their start and end apart: 4, of which 0 were waited for; matrix products, arithmetic and copies ran while one was open for 2% of the time, Pallas kernels for 12%

commit v1 on v0

v1 whole, which is shorter than its diff:
```python
import jax
import jax.numpy as jnp
from jax import lax
from jax.experimental import pallas as pl
from jax.experimental.layout import Layout, with_layout_constraint
from jax.experimental.pallas import tpu as pltpu
from jax.sharding import Mesh, PartitionSpec as P

F32 = jnp.float32
BF16 = jnp.bfloat16
VMEM_LIMIT = 56 * 1024 * 1024

ROWS = (0, 1, 2, 3, -1, 4, -2, 5)
PAD = 8
CHUNKS = 8
WIDE = 128


def dot_0(left, right):
    return lax.dot_general(left, right, (((0,), (0,)), ((), ())), preferred_element_type=F32)


def dot_t(left, right):
    return lax.dot_general(left, right, (((1,), (1,)), ((), ())), preferred_element_type=F32)


def dot_n(left, right):
    return jnp.dot(left, right, preferred_element_type=F32)


def iota(shape, dim):
    return lax.broadcasted_iota(jnp.int32, shape, dim)


def lane_is_low(rows):
    return iota((rows, 128), 1) < 64


def turn(value):
    return pltpu.roll(value, 64, 1)


def sigmoid(value):
    return 1.0 / (1.0 + jnp.exp(-value))


def stem_places(row, split):
    place = iota((512, 1), 0)
    tap = place // 64
    within = place % 64
    colour = (within >= 21).astype(jnp.int32) + (within >= 42).astype(jnp.int32)
    line = within - 21 * colour - (2 * row + 4)
    valid = (tap >= 1) & (within < 63) & (line >= 0) & (line <= 6)
    entry = line * 21 + (tap - 1) * 3 + colour
    if split:
        entry = jnp.where(entry < 128, entry, entry + 64)
    entry = jnp.where(valid, entry, -1)
    return (iota((512, 256), 1) == entry).astype(F32).astype(BF16)


def edges_kernel(tissue, cot, image, expand, up, down, order, wide, rows):
    step = pl.program_id(0)

    @pl.when(step == 0)
    def _():
        m, k = iota((128, 256), 0), iota((128, 256), 1)
        source = (m % 32) * 8 + ((m // 32) % 2) * 4 + (m // 64) * 3
        order[...] = (k == source).astype(F32).astype(BF16)
        both = jnp.concatenate([expand[...].astype(F32)] * 2, 0).T
        low = lane_is_low(256)
        wide[0:256, :] = jnp.where(low, both, 0.0).astype(BF16)
        wide[256:512, :] = jnp.where(low, 0.0, both).astype(BF16)

    for s in range(8):
        got = dot_n(order[...], cot[s * 256 : (s + 1) * 256, :]).astype(BF16)
        for n in range(4):
            rows[s * 32 : (s + 1) * 32, n * 128 : (n + 1) * 128] = got[n * 32 : (n + 1) * 32, :]
    back = dot_n(rows[...], wide[...]) * tissue[0, step].astype(F32)
    low = lane_is_low(128)
    a, b = back[0:128], back[128:256]
    first = jnp.where(low, a, turn(b)).astype(BF16)
    last = jnp.where(low, turn(a), b).astype(BF16)
    for v in range(4):
        up[0:32, v * 128 : (v + 1) * 128] = first[v * 32 : (v + 1) * 32, :]
        down[0:32, v * 128 : (v + 1) * 128] = last[v * 32 : (v + 1) * 32, :]
    for k in range(3):
        up[32 + 8 * k : 40 + 8 * k, :] = image[0, k]
        down[32 + 8 * k : 40 + 8 * k, :] = image[0, k]


def prepare_kernel(tissue, cot, expand, stem_t, conv_t, cot_f, back2, w1, w2, w2b, order, wide, filt):
    step = pl.program_id(0)

    @pl.when(step == 0)
    def _():
        m, k = iota((256, 256), 0), iota((256, 256), 1)
        source = (m % 32) * 8 + ((m // 32) % 2) * 4 + m // 64
        order[...] = (k == source).astype(F32).astype(BF16)
        wide[...] = jnp.zeros(wide.shape, BF16)
        both = jnp.concatenate([expand[...].astype(F32)] * 2, 0).T
        low = lane_is_low(256)
        for r in range(4):
            keep = low if r % 2 == 0 else jnp.logical_not(low)
            wide[r * 256 : (r + 1) * 256, (r // 2) * 128 : (r // 2 + 1) * 128] = jnp.where(keep, both, 0.0).astype(BF16)

    @pl.when(step == 1)
    def _():
        filt[...] = jnp.zeros(filt.shape, F32)
        filt[0:64, 0:147] = stem_t[...].astype(F32)
        both = filt[0:64, 0:256]
        both = jnp.concatenate([both, both], 0).T
        low = lane_is_low(256)
        halves = [jnp.where(low, both, 0.0).astype(BF16), jnp.where(low, 0.0, both).astype(BF16)]
        for t in range(4):
            tile = dot_n(stem_places(ROWS[2 * t], False), halves[0]) + dot_n(stem_places(ROWS[2 * t + 1], False), halves[1])
            w1[:, t * 128 : (t + 1) * 128] = tile.astype(BF16)

    @pl.when(step == 2)
    def _():
        filt[0:64, 0:576] = conv_t[...].astype(F32)
        filt[64:128, 0:576] = conv_t[...].astype(F32)
        turned = filt[...].T
        low = lane_is_low(64)
        flat = jnp.zeros((64, 128), F32)

        def pair(i0, i1, j):
            tiles = [turned[(3 * i + j) * 64 : (3 * i + j + 1) * 64, :] if 0 <= i <= 2 else flat for i in (i0, i1)]
            return jnp.where(low, tiles[0], tiles[1]).astype(BF16)

        for j in range(3):
            for a in range(8):
                base = j * 384 + a * 64 if a < 6 else 1152 + j * 128 + (a - 6) * 64
                for t in range(3):
                    i0, i1 = (ROWS[a] - ROWS[2 * t + e] + 1 for e in range(2))
                    w2[base : base + 64, t * 128 : (t + 1) * 128] = pair(i0, i1, j)

    @pl.when(step == 3)
    def _():
        blocks = [conv_t[:, n * 64 : (n + 1) * 64].astype(F32) for n in range(9)]
        empty = jnp.zeros((64, 64), F32)

        def block(i, j):
            return blocks[3 * i + j] if 0 <= i <= 2 else empty

        for j in range(3):
            for slot in range(6):
                for t in range(2):
                    tile = jnp.concatenate([block(2 * t + e - ROWS[slot] + 1, j) for e in range(2)], 1)
                    w2b[slot * 64 : (slot + 1) * 64, j * 256 + t * 128 : j * 256 + (t + 1) * 128] = tile.astype(BF16)

    for s in range(8):
        got = dot_n(order[...], cot[s * 256 : (s + 1) * 256, :]).astype(BF16)
        for n in range(8):
            cot_f[s * 32 : (s + 1) * 32, n * 128 : (n + 1) * 128] = got[n * 32 : (n + 1) * 32, :]
    back2[...] = dot_n(cot_f[...], wide[...]) * tissue[0, step].astype(F32)


def main_kernel(
    tissue, place, own_i, before_i, after_i, w1_i, w2_i, back2_i, w2b_i, cot_i, out_o, totals,
    own, before, after, w1, w2, back2, w2b, cot_f,
    lines, cols, z, act, slope1, act_sh, act2, grad2, wide, mixed, out, sems,
):
    count = [0]

    def fetch(src, dst):
        copy = pltpu.make_async_copy(src, dst, sems.at[count[0]])
        copy.start()
        count[0] += 1
        return copy

    in_image = [fetch(own_i, own), fetch(before_i, before), fetch(after_i, after)]
    in_w1 = fetch(w1_i, w1)
    in_w2 = fetch(w2_i, w2)
    in_back = [fetch(back2_i, back2), fetch(w2b_i, w2b)]
    in_cot = fetch(cot_i, cot_f)

    m, x = iota((128, 512), 0), iota((128, 512), 1)
    pick = (x == jnp.where(x < 256, 2 * m, 2 * m + 257)).astype(F32).astype(BF16)
    cols[0:PAD, :] = jnp.zeros((PAD, 128), F32)
    cols[PAD + 1024 :, :] = jnp.zeros((PAD, 128), F32)
    act[0:PAD, :] = jnp.zeros((PAD, 512), F32)
    act[PAD + 1024 :, :] = jnp.zeros((PAD, 512), F32)
    wide[0:PAD, :] = jnp.zeros((PAD, 768), F32)
    wide[PAD + 1024 :, :] = jnp.zeros((PAD, 768), F32)
    lines[63:64, :] = jnp.zeros((1, 2048), F32)
    none = jnp.zeros((64, 256), BF16)
    for copy in in_image:
        copy.wait()
    for k in range(3):
        lines[21 * k : 21 * k + 7, :] = before[32 + 8 * k : 40 + 8 * k, :].astype(F32)[1:8]
        lines[21 * k + 7 : 21 * k + 15, :] = own[0, k].astype(F32)
        lines[21 * k + 15 : 21 * k + 21, :] = after[32 + 8 * k : 40 + 8 * k, :].astype(F32)[0:6]
    for t in range(8):
        part = lines[:, t * 256 : (t + 1) * 256].astype(BF16)
        spread = jnp.concatenate([jnp.concatenate([part, none], 0), jnp.concatenate([none, part], 0)], 1)
        cols[PAD + t * 128 : PAD + (t + 1) * 128, :] = dot_t(pick, spread)

    ends = jnp.where(lane_is_low(1), place[0, 0].astype(F32), place[0, 1].astype(F32))
    in_w1.wait()
    for t in range(CHUNKS):
        at = t * WIDE
        wins = [cols[PAD + at + s : PAD + at + s + WIDE, :].astype(BF16) for s in (-2, -1, 0, 1)]
        zt = jnp.concatenate(wins, 1)
        z[at : at + WIDE, :] = zt
        pre = dot_n(zt, w1[...])
        sig = sigmoid(pre)
        value = pre * sig
        act[PAD + at : PAD + at + WIDE, 0:256] = value[:, :256]
        act[PAD + at : PAD + at + WIDE, 256:384] = value[:, 256:384] * ends
        act[PAD + at : PAD + at + WIDE, 384:512] = value[:, 384:512] * ends
        slope1[at : at + WIDE, :] = (sig * (1.0 + pre * (1.0 - sig)))[:, :256]

    low = lane_is_low(WIDE)
    in_w2.wait()
    for copy in in_back:
        copy.wait()
    for t in range(CHUNKS):
        at = t * WIDE
        wins = [act[PAD + at + j - 1 : PAD + at + j - 1 + WIDE, :].astype(BF16) for j in range(3)]
        near = jnp.concatenate([win[:, :384] for win in wins], 1)
        act_sh[at : at + WIDE, :] = near
        pre = dot_n(jnp.concatenate([near] + [win[:, 384:] for win in wins], 1), w2[...])
        sig = sigmoid(pre)
        keep = tissue[0, t // 2].astype(F32)
        act2[at : at + WIDE, :] = (pre * sig * keep)[:, :256].astype(BF16)
        slope = sig * (1.0 + pre * (1.0 - sig))
        grad2[at : at + WIDE, 0:256] = (back2[at : at + WIDE, :] * slope[:, :256]).astype(BF16)
        tiles = [(t // 2) * 4 + v for v in range(4)]
        a, b = (jnp.concatenate([ref[0:32, v * 128 : (v + 1) * 128] for v in tiles], 0).astype(F32) for ref in (before, after))
        ends = jnp.where(low, turn(a), b) if t % 2 else jnp.where(low, a, turn(b))
        grad2[at : at + WIDE, 256:384] = (ends * slope[:, 256:384]).astype(BF16)
        wide[PAD + at : PAD + at + WIDE, :] = dot_n(grad2[at : at + WIDE, :], w2b[...])

    for t in range(CHUNKS):
        at = t * WIDE
        back = wide[PAD + at + 1 : PAD + at + 1 + WIDE, 0:256] + wide[PAD + at : PAD + at + WIDE, 256:512]
        back = back + wide[PAD + at - 1 : PAD + at - 1 + WIDE, 512:768]
        gb = (back * slope1[at : at + WIDE, :]).astype(BF16)
        mixed[0, at : at + WIDE, :] = gb
        gr = gb.astype(F32)
        mixed[1, at : at + WIDE, :] = jnp.concatenate([turn(gr[:, :128]), turn(gr[:, 128:])], 1).astype(BF16)

    n, k = iota((256, 256), 0), iota((256, 256), 1)
    odd, r, two = n // 128, n % 4, (n % 128) // 4
    source = (r // 2) * 128 + ((r + odd) % 2) * 64 + 2 * two + odd
    order = (k == source).astype(F32).astype(BF16)
    for t in range(16):
        at = t * 64
        stack = jnp.concatenate([mixed[v, at : at + 64, u * 128 : (u + 1) * 128] for u in range(2) for v in range(2)], 0)
        got = dot_n(order, stack)
        out[t * 128 : (t + 1) * 128, :] = jnp.where(low, got[0:128], got[128:256]).astype(BF16)
    out_copy = fetch(out, out_o)

    scale = 1.0 / 1024.0
    low = lane_is_low(64)
    prod = dot_0(grad2[:, 0:256], act_sh[...]) * scale
    halves = {}
    for i in range(3):
        for j in range(3):
            at_low, at_high = [], []
            for r in range(4):
                slot = ROWS.index(r + i - 1)
                col = j * 384 + (slot // 2) * 128
                tile = prod[r * 64 : (r + 1) * 64, col : col + 128]
                (at_high if slot % 2 else at_low).append(tile)
            halves[3 * i + j] = (sum(at_low[1:], at_low[0]), sum(at_high[1:], at_high[0]))
    last = None
    for u in range(5):
        a, b = halves[2 * u]
        left = a + turn(b)
        if u == 4:
            last = left
        else:
            a, b = halves[2 * u + 1]
            totals[u * 64 : (u + 1) * 64, :] = jnp.where(low, left, turn(a) + b)

    in_cot.wait()
    total = None
    for t in range(2):
        both = dot_0(act2[:, t * 128 : (t + 1) * 128], cot_f[:, t * 512 : (t + 1) * 512])
        part = both[0:64, 0:256] + both[64:128, 256:512]
        total = part if total is None else total + part
    total = total * scale
    totals[320:384, :] = total[:, 0:128]
    totals[384:448, :] = total[:, 128:256]

    prod = dot_0(mixed[0], z[...]) * scale
    stem = None
    for r in range(4):
        part = prod[r * 64 : (r + 1) * 64, :]
        pieces = []
        for _ in range(3):
            piece = part.astype(BF16)
            pieces.append(piece)
            part = part - piece.astype(F32)
        term = dot_n(jnp.concatenate(pieces, 0), stem_places(r, True))
        term = term[0:64] + term[64:128] + term[128:192]
        stem = term if stem is None else stem + term
    totals[256:320, :] = jnp.where(low, last, stem[:, 128:256])
    totals[448:512, :] = stem[:, 0:128]
    out_copy.wait()


def unpack_kernel(totals, stem_t, conv_t, expand):
    for u in range(4):
        conv_t[:, u * 128 : (u + 1) * 128] = totals[u * 64 : (u + 1) * 64, :]
    mixed = totals[256:320, :]
    conv_t[:, 512:576] = mixed[:, 0:64]
    stem_t[:, 0:128] = totals[448:512, :]
    stem_t[:, 128:147] = turn(mixed)[:, 0:19]
    for u in range(2):
        expand[:, u * 128 : (u + 1) * 128] = totals[320 + u * 64 : 384 + u * 64, :]


def params():
    return pltpu.CompilerParams(vmem_limit_bytes=VMEM_LIMIT)


def shapes(*pairs):
    return [jax.ShapeDtypeStruct(shape, dtype) for shape, dtype in pairs]


SMEM = pl.BlockSpec(memory_space=pltpu.SMEM)
WHOLE = pl.BlockSpec(memory_space=pltpu.VMEM)
APART = pl.BlockSpec(memory_space=pl.ANY)


def prepare(tissue, cot, expand, stem_t, conv_t):
    def part(rows, lanes):
        return pl.BlockSpec((rows, lanes), lambda i: (i, 0))

    def fixed(rows, lanes):
        return pl.BlockSpec((rows, lanes), lambda i: (0, 0))

    return pl.pallas_call(
        prepare_kernel,
        grid=(4,),
        in_specs=[SMEM, part(2048, 128), fixed(64, 256), fixed(64, 147), fixed(64, 576)],
        out_specs=[part(256, 1024), part(256, 256), fixed(512, 512), fixed(1536, 384), fixed(384, 768)],
        out_shape=shapes(((1024, 1024), BF16), ((1024, 256), F32), ((512, 512), BF16), ((1536, 384), BF16), ((384, 768), BF16)),
        scratch_shapes=[pltpu.VMEM((256, 256), BF16), pltpu.VMEM((1024, 256), BF16), pltpu.VMEM((128, 640), F32)],
        compiler_params=params(),
        name="prepare",
    )(tissue, cot, expand, stem_t, conv_t)


def edges(tissue, cot, image, expand):
    return pl.pallas_call(
        edges_kernel,
        grid=(4,),
        in_specs=[
            SMEM,
            pl.BlockSpec((2048, 128), lambda i: (i, 0)),
            pl.BlockSpec((1, 3, 8, 512), lambda i: (0, 0, 0, i)),
            pl.BlockSpec((64, 256), lambda i: (0, 0)),
        ],
        out_specs=[pl.BlockSpec((56, 512), lambda i: (0, i))] * 2,
        out_shape=shapes(((56, 2048), BF16), ((56, 2048), BF16)),
        scratch_shapes=[pltpu.VMEM((128, 256), BF16), pltpu.VMEM((512, 128), BF16), pltpu.VMEM((256, 512), BF16)],
        compiler_params=params(),
        name="edges",
    )(tissue, cot, image, expand)


def main(tissue, place, own, before, after, w1, w2, back2, w2b, cot_f):
    return pl.pallas_call(
        main_kernel,
        in_specs=[SMEM, SMEM] + [APART] * 8,
        out_specs=[APART, WHOLE],
        out_shape=shapes(((2048, 128), BF16), ((512, 128), F32)),
        scratch_shapes=[
            pltpu.VMEM((1, 3, 8, 2048), BF16),
            pltpu.VMEM((56, 2048), BF16),
            pltpu.VMEM((56, 2048), BF16),
            pltpu.VMEM((512, 512), BF16),
            pltpu.VMEM((1536, 384), BF16),
            pltpu.VMEM((1024, 256), F32),
            pltpu.VMEM((384, 768), BF16),
            pltpu.VMEM((1024, 1024), BF16),
            pltpu.VMEM((64, 2048), F32),
            pltpu.VMEM((1024 + 2 * PAD, 128), F32),
            pltpu.VMEM((1024, 512), BF16),
            pltpu.VMEM((1024 + 2 * PAD, 512), F32),
            pltpu.VMEM((1024, 256), F32),
            pltpu.VMEM((1024, 1152), BF16),
            pltpu.VMEM((1024, 256), BF16),
            pltpu.VMEM((1024, 384), BF16),
            pltpu.VMEM((1024 + 2 * PAD, 768), F32),
            pltpu.VMEM((2, 1024, 256), BF16),
            pltpu.VMEM((2048, 128), BF16),
            pltpu.SemaphoreType.DMA((10,)),
        ],
        compiler_params=params(),
        name="main",
    )(tissue, place, own, before, after, w1, w2, back2, w2b, cot_f)


def unpack(totals):
    return pl.pallas_call(
        unpack_kernel,
        in_specs=[WHOLE],
        out_specs=[WHOLE] * 3,
        out_shape=shapes(((64, 147), F32), ((64, 576), F32), ((64, 256), F32)),
        compiler_params=params(),
        name="unpack",
    )(totals)


def reduce_all(totals):
    slide = ("x", "y", "core")
    count, depth = lax.axis_size(slide), lax.axis_size("tile")
    part = lax.all_to_all(totals.reshape(count, -1, 128), slide, 0, 0, tiled=True).sum(0)
    part = lax.all_to_all(jnp.broadcast_to(part[None], (depth,) + part.shape), "tile", 0, 0, tiled=True).sum(0)
    whole = lax.all_to_all(jnp.broadcast_to(part[None], (count,) + part.shape), slide, 0, 0, tiled=True)
    return whole.reshape(totals.shape)


def per_device(image, stem_weight, conv_weight, expand_weight, cotangent, tissue):
    depth = lax.axis_size("tile")
    position = lax.axis_index("tile")
    rows = tissue[0]
    cot = cotangent[0].reshape(4, 1024, 2, 128).transpose(1, 2, 0, 3).reshape(8192, 128)
    up, down = edges(rows, cot, image, expand_weight)
    before = lax.ppermute(down, "tile", [(i, i + 1) for i in range(depth - 1)])
    after = lax.ppermute(up, "tile", [(i + 1, i) for i in range(depth - 1)])
    place = jnp.stack([position > 0, position < depth - 1]).astype(jnp.int32)[None]
    cot_f, back2, w1, w2, w2b = prepare(rows, cot, expand_weight, stem_weight.T, conv_weight.T)
    out, totals = main(rows, place, image, before, after, w1, w2, back2, w2b, cot_f)
    stem_g, conv_g, expand_g = unpack(reduce_all(totals))
    field = out.reshape(512, 4, 128).transpose(1, 0, 2)
    field = with_layout_constraint(field, Layout(major_to_minor=(1, 0, 2)))
    return field.reshape(1, 4, 65536), stem_g.T, conv_g.T, expand_g


def solution(mesh):
    slide = ("x", "y", "core")
    fine = Mesh(mesh.devices.reshape(4, 4, 2, 8), slide + ("tile",))
    placed = (P(slide, None, "tile", None), P(), P(), P(), P(slide, "tile", None), P(slide, None, None))
    return jax.shard_map(
        per_device, mesh=fine, in_specs=placed, out_specs=(P(slide, "tile", None), P(), P(), P()), check_vma=False
    )
```

time: 92.2 us -> 80.8 us (0.88)
  starting transfers between devices: 11.8 us -> 5.66 us
  local copies, waits for them, and re-layouts: 3.72 us -> 0.8 us
  Pallas kernels: 26.8 us -> 24.4 us
    ppermute x4 -> x2, starting transfers between devices: 11.8 us -> 5.66 us  [the longest x1 4.37 us: per_device(): before = lax.ppermute(down, 'tile', [(i, i + 1) for i in range(depth - 1)])]
    pallas_call x5 -> x4, Pallas kernels: 26.8 us -> 24.4 us  [the longest x1 11.1 us: main(): pl.pallas_call(main_kernel, in_specs=[SMEM, SMEM] + [APART] * 8, out_spec...]
    pad x1 -> x0, local copies, waits for them, and re-layouts: 1.38 us -> none  [per_device(): stem_t = jnp.pad(stem_weight.T, ((0, 0), (0, 109)))]
    squeeze x1 -> x0, local copies, waits for them, and re-layouts: 0.99 us -> none  [per_device(): halo_b = lax.ppermute(edge[0], 'tile', up)]
  transfers between devices with their start and end apart: 4 -> 2, of which waited for: 0 -> 0; matrix products, arithmetic and copies ran while one was open for 2% -> 1% of each run, Pallas kernels for 12% -> 9%
where the time goes in v1:
time: 80.8 us; the launch traced here: 80.4 us
  blocking collectives  48.2 us (60%)
  Pallas kernels  24.4 us (30%)
  starting transfers between devices  5.66 us (7%)
    all_to_all x1, blocking collectives, reduce_all(): lax.all_to_all(totals.reshape(count, -1, 128), slide, 0, 0, tiled=True)  17.4 us
    all_to_all x1, blocking collectives, reduce_all(): lax.all_to_all(jnp.broadcast_to(part[None], (depth,) + part.shape), 'tile...  16.7 us
    all_to_all x1, blocking collectives, reduce_all(): lax.all_to_all(jnp.broadcast_to(part[None], (count,) + part.shape), slide...  14.1 us
    pallas_call x1, Pallas kernels, main(): pl.pallas_call(main_kernel, in_specs=[SMEM, SMEM] + [APART] * 8, out_spec...  11.1 us
    pallas_call x1, Pallas kernels, prepare(): pl.pallas_call(prepare_kernel, grid=(4,), in_specs=[SMEM, part(2048, 128)...  7 us
    pallas_call x1, Pallas kernels, edges(): pl.pallas_call(edges_kernel, grid=(4,), in_specs=[SMEM, pl.BlockSpec((204...  4.63 us
    ppermute x1, starting transfers between devices, per_device(): before = lax.ppermute(down, 'tile', [(i, i + 1) for i in range(depth - 1)])  4.37 us
    pallas_call x1, Pallas kernels, unpack(): pl.pallas_call(unpack_kernel, in_specs=[WHOLE], out_specs=[WHOLE] * 3, ou...  1.67 us
  transfers between devices with their start and end apart: 2, of which 0 were waited for; matrix products, arithmetic and copies ran while one was open for 1% of the time, Pallas kernels for 9%

profile of v1, /device:TPU:1, one launch (start us, length us, event | category | flops | bytes accessed | tf_op | source)
XLA Modules:
  0.0 80.4 jit_solution(16728345406812356046)
XLA Ops:
  0.6 4.6 %edges.1 = (bf16[56,2048]{1,0:T(8,128)(2,1)}, bf16[56,2048]{1,0:T(8,128)(2,1)}) custom-call(s32[1,4]{1,0:T(1,128)} %bitcast.25, bf16[8192,128]{1,0:T(8,128)(2,1)} %bitcast.19, bf16[1,3,8,2048]{3,2,1,0:T(8,128)(2,1)} %own_i.1, bf16[64,256]{1,0:T(8,128)(2,1)} %expand.3), custom_call_target="tpu_custom_call" | custom-call | tf_op jit(solution)/shard_map/edges/pallas_call | solution.py:348
  5.3 4.4 %collective-permute-start = (bf16[56,2048]{1,0:T(8,128)(2,1)}, bf16[56,2048]{1,0:T(8,128)(2,1)S(1)}, u32[]{:S(2)}, u32[]{:S(2)}) collective-permute-start(bf16[56,2048]{1,0:T(8,128)(2,1)} %get-tuple-element.16), channel_id=1, source_target_pairs={{0,1},{1,2},{2,3},{3,4},{4,5},{5,6},{6,7},{8,9},{9,10},{10,11},{11... | collective-permute-start | bytes 688136 | tf_op jit(solution)/shard_map/ppermute | solution.py:424
  9.6 1.3 %collective-permute-start.1 = (bf16[56,2048]{1,0:T(8,128)(2,1)}, bf16[56,2048]{1,0:T(8,128)(2,1)S(1)}, u32[]{:S(2)}, u32[]{:S(2)}) collective-permute-start(bf16[56,2048]{1,0:T(8,128)(2,1)} %get-tuple-element.17), channel_id=1, source_target_pairs={{1,0},{2,1},{3,2},{4,3},{5,4},{6,5},{7,6},{9,8},{10,9},{11,10},{12... | collective-permute-start | bytes 688136 | tf_op jit(solution)/shard_map/ppermute | solution.py:425
  11.0 7.0 %prepare.1 = (bf16[1024,1024]{1,0:T(8,128)(2,1)}, f32[1024,256]{1,0:T(8,128)}, bf16[512,512]{1,0:T(8,128)(2,1)}, bf16[1536,384]{1,0:T(8,128)(2,1)}, bf16[384,768]{1,0:T(8,128)(2,1)}) custom-call(s32[1,4]{1,0:T(1,128)} %bitcast.26, bf16[8192,128]{1,0:T(8,128)(2,1)} %bitcast.20, bf16[64,256]{1,0:T(8,128)(2,1)} %expand.3, bf16[64,147]{1,0:T(8,128)(2,1)} %bitcast.24, ...), custom_call_target="tpu_custom_call" | custom-call | tf_op jit(solution)/shard_map/prepare/pallas_call | solution.py:335
  17.9 0.6 add_convert_fusion.place
  18.5 0.0 collective-permute-done.before_i
  18.5 0.0 copy-start
  18.5 0.0 collective-permute-done.1.after_i
  18.5 0.0 copy-start.1
  18.6 0.7 copy-done
  19.2 0.1 copy-done.1
  19.3 11.1 %main.1 = (bf16[2048,128]{1,0:T(8,128)(2,1)}, f32[512,128]{1,0:T(8,128)}) custom-call(s32[1,4]{1,0:T(1,128)} %bitcast.27, s32[1,2]{1,0:T(1,128)} %add_convert_fusion.place, bf16[1,3,8,2048]{3,2,1,0:T(8,128)(2,1)} %own_i.1, bf16[56,2048]{1,0:T(8,128)(2,1)} %copy-done, bf16[56,2048]{1,0:T(8,128)(2,1)} %copy-done.1, bf16[512,512]{1,0:T(8,128)(2,1)} %get-tuple-element.18.w1_i, ...), custom_call_target="tpu_custom_call" | custom-call | tf_op jit(solution)/shard_map/main/pallas_call | solution.py:366
  30.4 17.4 %all_to_all.15 = f32[32,16,128]{2,1,0:T(8,128)S(1)} all-to-all(f32[32,16,128]{2,1,0:T(8,128)} %bitcast.22), channel_id=1, replica_groups=mesh['x'=4,'y'=4,'core'=2,'tile'=8] {'x','y','core'}, dimensions={0} | all-to-all | bytes 524288 | tf_op jit(solution)/shard_map/all_to_all | solution.py:412
  47.9 16.7 %all_to_all.16 = f32[8,16,128]{2,1,0:T(8,128)S(1)} all-to-all(f32[8,16,128]{2,1,0:T(8,128)S(1)} %broadcast_in_dim.4), channel_id=1, replica_groups=mesh['x'=4,'y'=4,'core'=2,'tile'=8] {'tile'}, dimensions={0} | all-to-all | bytes 131072 | tf_op jit(solution)/shard_map/all_to_all | solution.py:413
  64.6 14.1 %all_to_all.17 = f32[32,16,128]{2,1,0:T(8,128)} all-to-all(f32[32,16,128]{2,1,0:T(8,128)S(1)} %broadcast_in_dim.5), channel_id=1, replica_groups=mesh['x'=4,'y'=4,'core'=2,'tile'=8] {'x','y','core'}, dimensions={0} | all-to-all | bytes 524288 | tf_op jit(solution)/shard_map/all_to_all | solution.py:414
  78.7 1.7 %unpack.1 = (f32[64,147]{1,0:T(8,128)}, f32[64,576]{1,0:T(8,128)}, f32[64,256]{1,0:T(8,128)}) custom-call(f32[512,128]{1,0:T(8,128)} %bitcast.21), custom_call_target="tpu_custom_call" | custom-call | tf_op jit(solution)/shard_map/unpack/pallas_call | solution.py:399
  (4 shorter events, 0.1 us)
Async XLA Ops:
  5.3 13.3 %collective-permute-start = (bf16[56,2048]{1,0:T(8,128)(2,1)}, bf16[56,2048]{1,0:T(8,128)(2,1)S(1)}, u32[]{:S(2)}, u32[]{:S(2)}) collective-permute-start(bf16[56,2048]{1,0:T(8,128)(2,1)} %get-tuple-element.16), channel_id=1, source_target_pairs={{0,1},{1,2},{2,3},{3,4},{4,5},{5,6},{6,7},{8,9},{9,10},{10,11},{11... | collective-permute-start | bytes 688136 | tf_op jit(solution)/shard_map/ppermute | solution.py:424
  9.6 8.9 %collective-permute-start.1 = (bf16[56,2048]{1,0:T(8,128)(2,1)}, bf16[56,2048]{1,0:T(8,128)(2,1)S(1)}, u32[]{:S(2)}, u32[]{:S(2)}) collective-permute-start(bf16[56,2048]{1,0:T(8,128)(2,1)} %get-tuple-element.17), channel_id=1, source_target_pairs={{1,0},{2,1},{3,2},{4,3},{5,4},{6,5},{7,6},{9,8},{10,9},{11,10},{12... | collective-permute-start | bytes 688136 | tf_op jit(solution)/shard_map/ppermute | solution.py:425
  18.5 0.7 copy-start
  18.5 0.8 copy-start.1

commit v2 on v1

v2 whole, which is shorter than its diff:
```python
import jax
import jax.numpy as jnp
from jax import lax
from jax.experimental import pallas as pl
from jax.experimental.layout import Layout, with_layout_constraint
from jax.experimental.pallas import tpu as pltpu
from jax.sharding import Mesh, PartitionSpec as P

F32 = jnp.float32
BF16 = jnp.bfloat16
VMEM_LIMIT = 56 * 1024 * 1024

ROWS = (0, 1, 2, 3, -1, 4, -2, 5)
PAD = 8
CHUNKS = 8
WIDE = 128
SPAN = 256


def dot_0(left, right):
    return lax.dot_general(left, right, (((0,), (0,)), ((), ())), preferred_element_type=F32)


def dot_t(left, right):
    return lax.dot_general(left, right, (((1,), (1,)), ((), ())), preferred_element_type=F32)


def dot_n(left, right):
    return jnp.dot(left, right, preferred_element_type=F32)


def iota(shape, dim):
    return lax.broadcasted_iota(jnp.int32, shape, dim)


def lane_is_low(rows):
    return iota((rows, 128), 1) < 64


def turn(value):
    return pltpu.roll(value, 64, 1)


def sigmoid(value):
    return 1.0 / (1.0 + jnp.exp(-value))


def stem_places(row, split):
    place = iota((512, 1), 0)
    tap = place // 64
    within = place % 64
    colour = (within >= 21).astype(jnp.int32) + (within >= 42).astype(jnp.int32)
    line = within - 21 * colour - (2 * row + 4)
    valid = (tap >= 1) & (within < 63) & (line >= 0) & (line <= 6)
    entry = line * 21 + (tap - 1) * 3 + colour
    if split:
        entry = jnp.where(entry < 128, entry, entry + 64)
    entry = jnp.where(valid, entry, -1)
    return (iota((512, 256), 1) == entry).astype(F32).astype(BF16)


def is_even():
    return lax.axis_index("tile") % 2 == 0


def fetcher(sems):
    count = [0]

    def fetch(src, dst):
        copy = pltpu.make_async_copy(src, dst, sems.at[count[0]])
        copy.start()
        count[0] += 1
        return copy

    return fetch


def edges_kernel(tissue, cot_i, image, expand, to_first, to_second, cot, rows, sems):
    even = is_even()
    fetch = fetcher(sems)
    parts = [fetch(cot_i.at[pl.ds(q * 2048, 2048)], cot.at[pl.ds(q * 2048, 2048)]) for q in range(4)]
    for k in range(3):
        to_first[32 + 8 * k : 40 + 8 * k, :] = image[0, k]
        to_second[32 + 8 * k : 40 + 8 * k, :] = image[0, k]
    m, k = iota((128, 256), 0), iota((128, 256), 1)
    source = (m % 32) * 8 + ((m // 32) % 2) * 4 + (m // 64) * 3
    order = (k == source).astype(F32).astype(BF16)
    both = jnp.concatenate([expand[...].astype(F32)] * 2, 0).T
    low = lane_is_low(256)
    wide = jnp.concatenate([jnp.where(low, both, 0.0), jnp.where(low, 0.0, both)], 0).astype(BF16)
    low = lane_is_low(128)
    for q in range(4):
        parts[q].wait()
        for s in range(8):
            got = dot_n(order, cot[q * 2048 + s * 256 : q * 2048 + (s + 1) * 256, :]).astype(BF16)
            for n in range(4):
                rows[q * 256 + s * 32 : q * 256 + (s + 1) * 32, n * 128 : (n + 1) * 128] = got[n * 32 : (n + 1) * 32, :]
        back = dot_n(rows[q * 256 : (q + 1) * 256, :], wide) * tissue[0, q].astype(F32)
        a, b = back[0:128], back[128:256]
        top = jnp.where(low, a, turn(b))
        bottom = jnp.where(low, turn(a), b)
        first = jnp.where(even, bottom, top).astype(BF16)
        second = jnp.where(even, top, bottom).astype(BF16)
        for v in range(4):
            u = q * 4 + v
            to_first[0:32, u * 128 : (u + 1) * 128] = first[v * 32 : (v + 1) * 32, :]
            to_second[0:32, u * 128 : (u + 1) * 128] = second[v * 32 : (v + 1) * 32, :]


def prepare_kernel(
    tissue, cot_i, expand, stem_t, conv_t, cot_o, back2_o, w1_o, w2_o, w2b_o,
    cot, cot_f, back2, w1, w2, w2b, wide, filt, sems,
):
    fetch = fetcher(sems)
    parts = [fetch(cot_i.at[pl.ds(q * 2048, 2048)], cot.at[pl.ds(q * 2048, 2048)]) for q in range(4)]
    sent = []

    filt[...] = jnp.zeros(filt.shape, F32)
    filt[0:64, 0:147] = stem_t[...].astype(F32)
    both = filt[0:64, 0:256]
    both = jnp.concatenate([both, both], 0).T
    low = lane_is_low(256)
    halves = [jnp.where(low, both, 0.0).astype(BF16), jnp.where(low, 0.0, both).astype(BF16)]
    for t in range(4):
        tile = dot_n(stem_places(ROWS[2 * t], False), halves[0]) + dot_n(stem_places(ROWS[2 * t + 1], False), halves[1])
        w1[:, t * 128 : (t + 1) * 128] = tile.astype(BF16)
    sent.append(fetch(w1, w1_o))

    filt[0:64, 0:576] = conv_t[...].astype(F32)
    filt[64:128, 0:576] = conv_t[...].astype(F32)
    turned = filt[...].T
    low = lane_is_low(64)
    flat = jnp.zeros((64, 128), F32)

    def pair(i0, i1, j):
        tiles = [turned[(3 * i + j) * 64 : (3 * i + j + 1) * 64, :] if 0 <= i <= 2 else flat for i in (i0, i1)]
        return jnp.where(low, tiles[0], tiles[1]).astype(BF16)

    for j in range(3):
        for a in range(8):
            base = j * 384 + a * 64 if a < 6 else 1152 + j * 128 + (a - 6) * 64
            for t in range(3):
                i0, i1 = (ROWS[a] - ROWS[2 * t + e] + 1 for e in range(2))
                w2[base : base + 64, t * 128 : (t + 1) * 128] = pair(i0, i1, j)
    sent.append(fetch(w2, w2_o))
    blocks = [conv_t[:, n * 64 : (n + 1) * 64].astype(F32) for n in range(9)]
    empty = jnp.zeros((64, 64), F32)

    def block(i, j):
        return blocks[3 * i + j] if 0 <= i <= 2 else empty

    for j in range(3):
        for slot in range(6):
            for t in range(2):
                tile = jnp.concatenate([block(2 * t + e - ROWS[slot] + 1, j) for e in range(2)], 1)
                w2b[slot * 64 : (slot + 1) * 64, j * 256 + t * 128 : j * 256 + (t + 1) * 128] = tile.astype(BF16)
    sent.append(fetch(w2b, w2b_o))

    m, k = iota((256, 256), 0), iota((256, 256), 1)
    source = (m % 32) * 8 + ((m // 32) % 2) * 4 + m // 64
    order = (k == source).astype(F32).astype(BF16)
    wide[...] = jnp.zeros(wide.shape, BF16)
    both = jnp.concatenate([expand[...].astype(F32)] * 2, 0).T
    low = lane_is_low(256)
    for r in range(4):
        keep = low if r % 2 == 0 else jnp.logical_not(low)
        wide[r * 256 : (r + 1) * 256, (r // 2) * 128 : (r // 2 + 1) * 128] = jnp.where(keep, both, 0.0).astype(BF16)
    for q in range(4):
        parts[q].wait()
        for s in range(8):
            got = dot_n(order, cot[q * 2048 + s * 256 : q * 2048 + (s + 1) * 256, :]).astype(BF16)
            for n in range(8):
                cot_f[q * 256 + s * 32 : q * 256 + (s + 1) * 32, n * 128 : (n + 1) * 128] = got[n * 32 : (n + 1) * 32, :]
        part = pl.ds(q * 256, 256)
        back2[part, :] = dot_n(cot_f[part, :], wide[...]) * tissue[0, q].astype(F32)
        sent.append(fetch(cot_f.at[part], cot_o.at[part]))
        sent.append(fetch(back2.at[part], back2_o.at[part]))
    for copy in sent:
        copy.wait()


def main_kernel(
    tissue, own_i, first_i, second_i, w1_i, w2_i, back2_i, w2b_i, cot_i, out_o, totals,
    own, before, after, w1, w2, back2, w2b, cot_f,
    lines, cols, z, act, slope1, act_sh, act2, grad2, wide, mixed, out, sems,
):
    fetch = fetcher(sems)
    even = is_even()

    @pl.when(even)
    def _():
        pltpu.make_async_copy(second_i, before, sems.at[8]).start()
        pltpu.make_async_copy(first_i, after, sems.at[9]).start()

    @pl.when(jnp.logical_not(even))
    def _():
        pltpu.make_async_copy(first_i, before, sems.at[8]).start()
        pltpu.make_async_copy(second_i, after, sems.at[9]).start()

    in_image = [fetch(own_i, own)]
    in_image += [pltpu.make_async_copy(first_i, before, sems.at[8]), pltpu.make_async_copy(second_i, after, sems.at[9])]
    in_w1 = fetch(w1_i, w1)
    in_w2 = fetch(w2_i, w2)
    in_back = [fetch(back2_i, back2), fetch(w2b_i, w2b)]
    in_cot = fetch(cot_i, cot_f)

    m, x = iota((128, 512), 0), iota((128, 512), 1)
    pick = (x == jnp.where(x < 256, 2 * m, 2 * m + 257)).astype(F32).astype(BF16)
    cols[0:PAD, :] = jnp.zeros((PAD, 128), F32)
    cols[PAD + 1024 :, :] = jnp.zeros((PAD, 128), F32)
    act[0:PAD, :] = jnp.zeros((PAD, 512), F32)
    act[PAD + 1024 :, :] = jnp.zeros((PAD, 512), F32)
    wide[0:PAD, :] = jnp.zeros((PAD, 768), F32)
    wide[PAD + 1024 :, :] = jnp.zeros((PAD, 768), F32)
    lines[63:64, :] = jnp.zeros((1, 2048), F32)
    none = jnp.zeros((64, 256), BF16)
    for copy in in_image:
        copy.wait()
    for k in range(3):
        lines[21 * k : 21 * k + 7, :] = before[32 + 8 * k : 40 + 8 * k, :].astype(F32)[1:8]
        lines[21 * k + 7 : 21 * k + 15, :] = own[0, k].astype(F32)
        lines[21 * k + 15 : 21 * k + 21, :] = after[32 + 8 * k : 40 + 8 * k, :].astype(F32)[0:6]
    for t in range(8):
        part = lines[:, t * 256 : (t + 1) * 256].astype(BF16)
        spread = jnp.concatenate([jnp.concatenate([part, none], 0), jnp.concatenate([none, part], 0)], 1)
        cols[PAD + t * 128 : PAD + (t + 1) * 128, :] = dot_t(pick, spread)

    position = lax.axis_index("tile")
    ends = jnp.where(lane_is_low(1), (position > 0).astype(F32), (position < lax.axis_size("tile") - 1).astype(F32))
    in_w1.wait()
    for t in range(CHUNKS):
        at = t * WIDE
        wins = [cols[PAD + at + s : PAD + at + s + WIDE, :].astype(BF16) for s in (-2, -1, 0, 1)]
        zt = jnp.concatenate(wins, 1)
        z[at : at + WIDE, :] = zt
        pre = dot_n(zt, w1[...])
        sig = sigmoid(pre)
        value = pre * sig
        act[PAD + at : PAD + at + WIDE, 0:256] = value[:, :256]
        act[PAD + at : PAD + at + WIDE, 256:384] = value[:, 256:384] * ends
        act[PAD + at : PAD + at + WIDE, 384:512] = value[:, 384:512] * ends
        slope1[at : at + WIDE, :] = (sig * (1.0 + pre * (1.0 - sig)))[:, :256]

    low = lane_is_low(128)
    in_w2.wait()
    for copy in in_back:
        copy.wait()
    for t in range(1024 // SPAN):
        at = t * SPAN
        wins = [act[PAD + at + j - 1 : PAD + at + j - 1 + SPAN, :].astype(BF16) for j in range(3)]
        near = jnp.concatenate([win[:, :384] for win in wins], 1)
        act_sh[at : at + SPAN, :] = near
        pre = dot_n(near, w2[0:1152, 0:256])
        sig = sigmoid(pre)
        keep = tissue[0, at // 256].astype(F32)
        act2[at : at + SPAN, :] = (pre * sig * keep).astype(BF16)
        grad2[at : at + SPAN, 0:256] = (back2[at : at + SPAN, :] * (sig * (1.0 + pre * (1.0 - sig)))).astype(BF16)
        pre = dot_n(jnp.concatenate([near] + [win[:, 384:] for win in wins], 1), w2[:, 256:384])
        sig = sigmoid(pre)
        ends = []
        for u in range(at // 128, (at + SPAN) // 128):
            tiles = [(u // 2) * 4 + v for v in range(4)]
            a, b = (jnp.concatenate([ref[0:32, v * 128 : (v + 1) * 128] for v in tiles], 0).astype(F32) for ref in (before, after))
            ends.append(jnp.where(low, turn(a), b) if u % 2 else jnp.where(low, a, turn(b)))
        slope = sig * (1.0 + pre * (1.0 - sig))
        grad2[at : at + SPAN, 256:384] = (jnp.concatenate(ends, 0) * slope).astype(BF16)
        wide[PAD + at : PAD + at + SPAN, :] = dot_n(grad2[at : at + SPAN, :], w2b[...])

    for t in range(CHUNKS):
        at = t * WIDE
        back = wide[PAD + at + 1 : PAD + at + 1 + WIDE, 0:256] + wide[PAD + at : PAD + at + WIDE, 256:512]
        back = back + wide[PAD + at - 1 : PAD + at - 1 + WIDE, 512:768]
        gb = (back * slope1[at : at + WIDE, :]).astype(BF16)
        mixed[0, at : at + WIDE, :] = gb
        gr = gb.astype(F32)
        mixed[1, at : at + WIDE, :] = jnp.concatenate([turn(gr[:, :128]), turn(gr[:, 128:])], 1).astype(BF16)

    n, k = iota((256, 256), 0), iota((256, 256), 1)
    odd, r, two = n // 128, n % 4, (n % 128) // 4
    source = (r // 2) * 128 + ((r + odd) % 2) * 64 + 2 * two + odd
    order = (k == source).astype(F32).astype(BF16)
    for t in range(8):
        stacks = []
        for at in (t * 128, t * 128 + 64):
            stacks.append(jnp.concatenate([mixed[v, at : at + 64, u * 128 : (u + 1) * 128] for u in range(2) for v in range(2)], 0))
        got = dot_n(order, jnp.concatenate(stacks, 1))
        for e in range(2):
            at = t * 256 + e * 128
            out[at : at + 128, :] = jnp.where(low, got[0:128, e * 128 : e * 128 + 128], got[128:256, e * 128 : e * 128 + 128]).astype(BF16)
    out_copy = fetch(out, out_o)

    scale = 1.0 / 1024.0
    low = lane_is_low(64)
    prod = dot_0(grad2[:, 0:256], act_sh[...]) * scale
    halves = {}
    for i in range(3):
        for j in range(3):
            at_low, at_high = [], []
            for r in range(4):
                slot = ROWS.index(r + i - 1)
                col = j * 384 + (slot // 2) * 128
                tile = prod[r * 64 : (r + 1) * 64, col : col + 128]
                (at_high if slot % 2 else at_low).append(tile)
            halves[3 * i + j] = (sum(at_low[1:], at_low[0]), sum(at_high[1:], at_high[0]))
    last = None
    for u in range(5):
        a, b = halves[2 * u]
        left = a + turn(b)
        if u == 4:
            last = left
        else:
            a, b = halves[2 * u + 1]
            totals[u * 64 : (u + 1) * 64, :] = jnp.where(low, left, turn(a) + b)

    in_cot.wait()
    total = None
    for t in range(2):
        both = dot_0(act2[:, t * 128 : (t + 1) * 128], cot_f[:, t * 512 : (t + 1) * 512])
        part = both[0:64, 0:256] + both[64:128, 256:512]
        total = part if total is None else total + part
    total = total * scale
    totals[320:384, :] = total[:, 0:128]
    totals[384:448, :] = total[:, 128:256]

    prod = dot_0(mixed[0], z[...]) * scale
    stem = None
    for r in range(4):
        part = prod[r * 64 : (r + 1) * 64, :]
        pieces = []
        for _ in range(3):
            piece = part.astype(BF16)
            pieces.append(piece)
            part = part - piece.astype(F32)
        term = dot_n(jnp.concatenate(pieces, 0), stem_places(r, True))
        term = term[0:64] + term[64:128] + term[128:192]
        stem = term if stem is None else stem + term
    totals[256:320, :] = jnp.where(low, last, stem[:, 128:256])
    totals[448:512, :] = stem[:, 0:128]
    out_copy.wait()


def unpack_kernel(totals, stem_t, conv_t, expand):
    for u in range(4):
        conv_t[:, u * 128 : (u + 1) * 128] = totals[u * 64 : (u + 1) * 64, :]
    mixed = totals[256:320, :]
    conv_t[:, 512:576] = mixed[:, 0:64]
    stem_t[:, 0:128] = totals[448:512, :]
    stem_t[:, 128:147] = turn(mixed)[:, 0:19]
    for u in range(2):
        expand[:, u * 128 : (u + 1) * 128] = totals[320 + u * 64 : 384 + u * 64, :]


def params():
    return pltpu.CompilerParams(vmem_limit_bytes=VMEM_LIMIT)


def shapes(*pairs):
    return [jax.ShapeDtypeStruct(shape, dtype) for shape, dtype in pairs]


SMEM = pl.BlockSpec(memory_space=pltpu.SMEM)
WHOLE = pl.BlockSpec(memory_space=pltpu.VMEM)
APART = pl.BlockSpec(memory_space=pl.ANY)


def prepare(tissue, cot, expand, stem_t, conv_t):
    outs = (((1024, 1024), BF16), ((1024, 256), F32), ((512, 512), BF16), ((1536, 384), BF16), ((384, 768), BF16))
    return pl.pallas_call(
        prepare_kernel,
        in_specs=[SMEM, APART, WHOLE, WHOLE, WHOLE],
        out_specs=[APART] * 5,
        out_shape=shapes(*outs),
        scratch_shapes=[pltpu.VMEM((8192, 128), BF16)]
        + [pltpu.VMEM(shape, dtype) for shape, dtype in outs]
        + [pltpu.VMEM((1024, 256), BF16), pltpu.VMEM((128, 640), F32), pltpu.SemaphoreType.DMA((15,))],
        compiler_params=params(),
        name="prepare",
    )(tissue, cot, expand, stem_t, conv_t)


def edges(tissue, cot, image, expand):
    return pl.pallas_call(
        edges_kernel,
        in_specs=[SMEM, APART, WHOLE, WHOLE],
        out_specs=[WHOLE] * 2,
        out_shape=shapes(((56, 2048), BF16), ((56, 2048), BF16)),
        scratch_shapes=[pltpu.VMEM((8192, 128), BF16), pltpu.VMEM((1024, 512), BF16), pltpu.SemaphoreType.DMA((4,))],
        compiler_params=params(),
        name="edges",
    )(tissue, cot, image, expand)


def main(tissue, own, first, second, w1, w2, back2, w2b, cot_f):
    return pl.pallas_call(
        main_kernel,
        in_specs=[SMEM] + [APART] * 8,
        out_specs=[APART, WHOLE],
        out_shape=shapes(((2048, 128), BF16), ((512, 128), F32)),
        scratch_shapes=[
            pltpu.VMEM((1, 3, 8, 2048), BF16),
            pltpu.VMEM((56, 2048), BF16),
            pltpu.VMEM((56, 2048), BF16),
            pltpu.VMEM((512, 512), BF16),
            pltpu.VMEM((1536, 384), BF16),
            pltpu.VMEM((1024, 256), F32),
            pltpu.VMEM((384, 768), BF16),
            pltpu.VMEM((1024, 1024), BF16),
            pltpu.VMEM((64, 2048), F32),
            pltpu.VMEM((1024 + 2 * PAD, 128), F32),
            pltpu.VMEM((1024, 512), BF16),
            pltpu.VMEM((1024 + 2 * PAD, 512), F32),
            pltpu.VMEM((1024, 256), F32),
            pltpu.VMEM((1024, 1152), BF16),
            pltpu.VMEM((1024, 256), BF16),
            pltpu.VMEM((1024, 384), BF16),
            pltpu.VMEM((1024 + 2 * PAD, 768), F32),
            pltpu.VMEM((2, 1024, 256), BF16),
            pltpu.VMEM((2048, 128), BF16),
            pltpu.SemaphoreType.DMA((10,)),
        ],
        compiler_params=params(),
        name="main",
    )(tissue, own, first, second, w1, w2, back2, w2b, cot_f)


def unpack(totals):
    return pl.pallas_call(
        unpack_kernel,
        in_specs=[WHOLE],
        out_specs=[WHOLE] * 3,
        out_shape=shapes(((64, 147), F32), ((64, 576), F32), ((64, 256), F32)),
        compiler_params=params(),
        name="unpack",
    )(totals)


def reduce_all(totals):
    slide = ("x", "y", "core")
    count, depth = lax.axis_size(slide), lax.axis_size("tile")
    part = lax.all_to_all(totals.reshape(count, -1, 128), slide, 0, 0, tiled=True).sum(0)
    part = lax.all_to_all(jnp.broadcast_to(part[None], (depth,) + part.shape), "tile", 0, 0, tiled=True).sum(0)
    whole = lax.all_to_all(jnp.broadcast_to(part[None], (count,) + part.shape), slide, 0, 0, tiled=True)
    return whole.reshape(totals.shape)


def per_device(image, stem_weight, conv_weight, expand_weight, cotangent, tissue):
    depth = lax.axis_size("tile")
    rows = tissue[0]
    cot = cotangent[0].reshape(4, 1024, 2, 128).transpose(1, 2, 0, 3).reshape(8192, 128)
    first, second = edges(rows, cot, image, expand_weight)
    pairs = [[(i, i + 1) for i in range(start, depth - 1, 2)] for start in (0, 1)]
    first = lax.ppermute(first, "tile", pairs[0] + [(b, a) for a, b in pairs[0]])
    second = lax.ppermute(second, "tile", pairs[1] + [(b, a) for a, b in pairs[1]])
    cot_f, back2, w1, w2, w2b = prepare(rows, cot, expand_weight, stem_weight.T, conv_weight.T)
    out, totals = main(rows, image, first, second, w1, w2, back2, w2b, cot_f)
    stem_g, conv_g, expand_g = unpack(reduce_all(totals))
    field = out.reshape(512, 4, 128).transpose(1, 0, 2)
    field = with_layout_constraint(field, Layout(major_to_minor=(1, 0, 2)))
    return field.reshape(1, 4, 65536), stem_g.T, conv_g.T, expand_g


def solution(mesh):
    slide = ("x", "y", "core")
    fine = Mesh(mesh.devices.reshape(4, 4, 2, 8), slide + ("tile",))
    placed = (P(slide, None, "tile", None), P(), P(), P(), P(slide, "tile", None), P(slide, None, None))
    return jax.shard_map(
        per_device, mesh=fine, in_specs=placed, out_specs=(P(slide, "tile", None), P(), P(), P()), check_vma=False
    )
```

time: 80.8 us -> 77.1 us (0.954)
  starting transfers between devices: 5.66 us -> 3.22 us
  Pallas kernels: 24.4 us -> 23.1 us
    ppermute x2, starting transfers between devices: 5.66 us -> 3.22 us  [the longest x1 2.55 us: per_device(): lax.ppermute(first, 'tile', pairs[0] + [(b, a) for a, b in pairs[0]])]
    pallas_call x3, Pallas kernels: 22.7 us -> 21.5 us  [the longest x1 10.4 us: main(): pl.pallas_call(main_kernel, in_specs=[SMEM] + [APART] * 8, out_specs=[APA...]
    all_to_all x1, blocking collectives: 16.7 us -> 17.7 us  [reduce_all(): lax.all_to_all(jnp.broadcast_to(part[None], (depth,) + part.shape), 'tile...]
  transfers between devices with their start and end apart: 2 -> 2, of which waited for: 0 -> 0; matrix products, arithmetic and copies ran while one was open for 1% -> 0% of each run, Pallas kernels for 9% -> 8%
where the time goes in v2:
time: 77.1 us; the launch traced here: 76.7 us
  blocking collectives  48.8 us (63%)
  Pallas kernels  23.1 us (30%)
  starting transfers between devices  3.22 us (4%)
  local copies, waits for them, and re-layouts  0.78 us (1%)
    all_to_all x1, blocking collectives, reduce_all(): lax.all_to_all(jnp.broadcast_to(part[None], (depth,) + part.shape), 'tile...  17.7 us
    all_to_all x1, blocking collectives, reduce_all(): lax.all_to_all(totals.reshape(count, -1, 128), slide, 0, 0, tiled=True)  17 us
    all_to_all x1, blocking collectives, reduce_all(): lax.all_to_all(jnp.broadcast_to(part[None], (count,) + part.shape), slide...  14.1 us
    pallas_call x1, Pallas kernels, main(): pl.pallas_call(main_kernel, in_specs=[SMEM] + [APART] * 8, out_specs=[APA...  10.4 us
    pallas_call x1, Pallas kernels, prepare(): pl.pallas_call(prepare_kernel, in_specs=[SMEM, APART, WHOLE, WHOLE, WHOLE...  6.2 us
    pallas_call x1, Pallas kernels, edges(): pl.pallas_call(edges_kernel, in_specs=[SMEM, APART, WHOLE, WHOLE], out_sp...  4.85 us
    ppermute x1, starting transfers between devices, per_device(): lax.ppermute(first, 'tile', pairs[0] + [(b, a) for a, b in pairs[0]])  2.55 us
    pallas_call x1, Pallas kernels, unpack(): pl.pallas_call(unpack_kernel, in_specs=[WHOLE], out_specs=[WHOLE] * 3, ou...  1.67 us
  transfers between devices with their start and end apart: 2, of which 0 were waited for; matrix products, arithmetic and copies ran while one was open for 0% of the time, Pallas kernels for 8%

profile of v2, /device:TPU:1, one launch (start us, length us, event | category | flops | bytes accessed | tf_op | source)
XLA Modules:
  0.0 76.7 jit_solution(6320495516670075485)
XLA Ops:
  0.6 4.9 %edges.1 = (bf16[56,2048]{1,0:T(8,128)(2,1)}, bf16[56,2048]{1,0:T(8,128)(2,1)}) custom-call(s32[1,4]{1,0:T(1,128)} %bitcast.23, bf16[8192,128]{1,0:T(8,128)(2,1)} %bitcast.17, bf16[1,3,8,2048]{3,2,1,0:T(8,128)(2,1)} %own_i.1, bf16[64,256]{1,0:T(8,128)(2,1)} %expand.3), custom_call_target="tpu_custom_call" | custom-call | tf_op jit(solution)/shard_map/edges/pallas_call | solution.py:382
  5.5 2.6 %collective-permute-start = (bf16[56,2048]{1,0:T(8,128)(2,1)}, bf16[56,2048]{1,0:T(8,128)(2,1)S(1)}, u32[]{:S(2)}, u32[]{:S(2)}) collective-permute-start(bf16[56,2048]{1,0:T(8,128)(2,1)} %get-tuple-element.16), channel_id=1, source_target_pairs={{0,1},{2,3},{4,5},{6,7},{1,0},{3,2},{5,4},{7,6},{8,9},{10,11},{12,... | collective-permute-start | bytes 688136 | tf_op jit(solution)/shard_map/ppermute | solution.py:452
  8.0 0.7 collective-permute-start.1
  8.7 6.2 %prepare.1 = (bf16[1024,1024]{1,0:T(8,128)(2,1)}, f32[1024,256]{1,0:T(8,128)}, bf16[512,512]{1,0:T(8,128)(2,1)}, bf16[1536,384]{1,0:T(8,128)(2,1)}, bf16[384,768]{1,0:T(8,128)(2,1)}) custom-call(s32[1,4]{1,0:T(1,128)} %bitcast.24, bf16[8192,128]{1,0:T(8,128)(2,1)} %bitcast.18, bf16[64,256]{1,0:T(8,128)(2,1)} %expand.3, bf16[64,147]{1,0:T(8,128)(2,1)} %bitcast.22, ...), custom_call_target="tpu_custom_call" | custom-call | tf_op jit(solution)/shard_map/prepare/pallas_call | solution.py:368
  14.9 0.0 collective-permute-done.first_i
  14.9 0.0 copy-start
  14.9 0.0 collective-permute-done.1.second_i
  15.0 0.0 copy-start.1
  15.0 0.7 copy-done
  15.6 0.1 copy-done.1
  15.7 10.4 %main.1 = (bf16[2048,128]{1,0:T(8,128)(2,1)}, f32[512,128]{1,0:T(8,128)}) custom-call(s32[1,4]{1,0:T(1,128)} %bitcast.25, bf16[1,3,8,2048]{3,2,1,0:T(8,128)(2,1)} %own_i.1, bf16[56,2048]{1,0:T(8,128)(2,1)} %copy-done, bf16[56,2048]{1,0:T(8,128)(2,1)} %copy-done.1, bf16[512,512]{1,0:T(8,128)(2,1)} %get-tuple-element.18.w1_i, ...), custom_call_target="tpu_custom_call" | custom-call | tf_op jit(solution)/shard_map/main/pallas_call | solution.py:394
  26.1 17.0 %all_to_all.15 = f32[32,16,128]{2,1,0:T(8,128)S(1)} all-to-all(f32[32,16,128]{2,1,0:T(8,128)} %bitcast.20), channel_id=1, replica_groups=mesh['x'=4,'y'=4,'core'=2,'tile'=8] {'x','y','core'}, dimensions={0} | all-to-all | bytes 524288 | tf_op jit(solution)/shard_map/all_to_all | solution.py:440
  43.2 17.7 %all_to_all.16 = f32[8,16,128]{2,1,0:T(8,128)S(1)} all-to-all(f32[8,16,128]{2,1,0:T(8,128)S(1)} %broadcast_in_dim.4), channel_id=1, replica_groups=mesh['x'=4,'y'=4,'core'=2,'tile'=8] {'tile'}, dimensions={0} | all-to-all | bytes 131072 | tf_op jit(solution)/shard_map/all_to_all | solution.py:441
  60.9 14.1 %all_to_all.17 = f32[32,16,128]{2,1,0:T(8,128)} all-to-all(f32[32,16,128]{2,1,0:T(8,128)S(1)} %broadcast_in_dim.5), channel_id=1, replica_groups=mesh['x'=4,'y'=4,'core'=2,'tile'=8] {'x','y','core'}, dimensions={0} | all-to-all | bytes 524288 | tf_op jit(solution)/shard_map/all_to_all | solution.py:442
  75.0 1.7 %unpack.1 = (f32[64,147]{1,0:T(8,128)}, f32[64,576]{1,0:T(8,128)}, f32[64,256]{1,0:T(8,128)}) custom-call(f32[512,128]{1,0:T(8,128)} %bitcast.19), custom_call_target="tpu_custom_call" | custom-call | tf_op jit(solution)/shard_map/unpack/pallas_call | solution.py:427
  (4 shorter events, 0.1 us)
Async XLA Ops:
  5.5 9.4 %collective-permute-start = (bf16[56,2048]{1,0:T(8,128)(2,1)}, bf16[56,2048]{1,0:T(8,128)(2,1)S(1)}, u32[]{:S(2)}, u32[]{:S(2)}) collective-permute-start(bf16[56,2048]{1,0:T(8,128)(2,1)} %get-tuple-element.16), channel_id=1, source_target_pairs={{0,1},{2,3},{4,5},{6,7},{1,0},{3,2},{5,4},{7,6},{8,9},{10,11},{12,... | collective-permute-start | bytes 688136 | tf_op jit(solution)/shard_map/ppermute | solution.py:452
  8.0 6.9 %collective-permute-start.1 = (bf16[56,2048]{1,0:T(8,128)(2,1)}, bf16[56,2048]{1,0:T(8,128)(2,1)S(1)}, u32[]{:S(2)}, u32[]{:S(2)}) collective-permute-start(bf16[56,2048]{1,0:T(8,128)(2,1)} %get-tuple-element.17), channel_id=1, source_target_pairs={{1,2},{3,4},{5,6},{2,1},{4,3},{6,5},{9,10},{11,12},{13,14},{10,9},... | collective-permute-start | bytes 688136 | tf_op jit(solution)/shard_map/ppermute | solution.py:453
  14.9 0.7 copy-start
  15.0 0.8 copy-start.1

commit v3 on v2

--- a/solution.py
+++ b/solution.py
@@ -8,7 +8,7 @@
 
 F32 = jnp.float32
 BF16 = jnp.bfloat16
-VMEM_LIMIT = 56 * 1024 * 1024
+VMEM_LIMIT = 32 * 1024 * 1024
 
 ROWS = (0, 1, 2, 3, -1, 4, -2, 5)
 PAD = 8
@@ -75,16 +75,16 @@
     return fetch
 
 
-def edges_kernel(tissue, cot_i, image, expand, to_first, to_second, cot, rows, sems):
+def edges_kernel(tissue, cot_i, image_i, expand_i, to_first, to_second, cot, image, expand, rows, sems):
     even = is_even()
     fetch = fetcher(sems)
+    in_expand = fetch(expand_i, expand)
     parts = [fetch(cot_i.at[pl.ds(q * 2048, 2048)], cot.at[pl.ds(q * 2048, 2048)]) for q in range(4)]
-    for k in range(3):
-        to_first[32 + 8 * k : 40 + 8 * k, :] = image[0, k]
-        to_second[32 + 8 * k : 40 + 8 * k, :] = image[0, k]
+    in_image = fetch(image_i, image)
     m, k = iota((128, 256), 0), iota((128, 256), 1)
     source = (m % 32) * 8 + ((m // 32) % 2) * 4 + (m // 64) * 3
     order = (k == source).astype(F32).astype(BF16)
+    in_expand.wait()
     both = jnp.concatenate([expand[...].astype(F32)] * 2, 0).T
     low = lane_is_low(256)
     wide = jnp.concatenate([jnp.where(low, both, 0.0), jnp.where(low, 0.0, both)], 0).astype(BF16)
@@ -105,15 +105,15 @@
             u = q * 4 + v
             to_first[0:32, u * 128 : (u + 1) * 128] = first[v * 32 : (v + 1) * 32, :]
             to_second[0:32, u * 128 : (u + 1) * 128] = second[v * 32 : (v + 1) * 32, :]
-
-
-def prepare_kernel(
-    tissue, cot_i, expand, stem_t, conv_t, cot_o, back2_o, w1_o, w2_o, w2b_o,
-    cot, cot_f, back2, w1, w2, w2b, wide, filt, sems,
-):
+    in_image.wait()
+    for k in range(3):
+        to_first[32 + 8 * k : 40 + 8 * k, :] = image[0, k]
+        to_second[32 + 8 * k : 40 + 8 * k, :] = image[0, k]
+
+
+def prepare_kernel(tissue, cot_i, expand, stem_t, conv_t, cot_f, back2, w1, w2, w2b, cot, wide, filt, sems):
     fetch = fetcher(sems)
     parts = [fetch(cot_i.at[pl.ds(q * 2048, 2048)], cot.at[pl.ds(q * 2048, 2048)]) for q in range(4)]
-    sent = []
 
     filt[...] = jnp.zeros(filt.shape, F32)
     filt[0:64, 0:147] = stem_t[...].astype(F32)
@@ -124,7 +124,6 @@
     for t in range(4):
         tile = dot_n(stem_places(ROWS[2 * t], False), halves[0]) + dot_n(stem_places(ROWS[2 * t + 1], False), halves[1])
         w1[:, t * 128 : (t + 1) * 128] = tile.astype(BF16)
-    sent.append(fetch(w1, w1_o))
 
     filt[0:64, 0:576] = conv_t[...].astype(F32)
     filt[64:128, 0:576] = conv_t[...].astype(F32)
@@ -142,7 +141,6 @@
             for t in range(3):
                 i0, i1 = (ROWS[a] - ROWS[2 * t + e] + 1 for e in range(2))
                 w2[base : base + 64, t * 128 : (t + 1) * 128] = pair(i0, i1, j)
-    sent.append(fetch(w2, w2_o))
     blocks = [conv_t[:, n * 64 : (n + 1) * 64].astype(F32) for n in range(9)]
     empty = jnp.zeros((64, 64), F32)
 
@@ -154,7 +152,6 @@
             for t in range(2):
                 tile = jnp.concatenate([block(2 * t + e - ROWS[slot] + 1, j) for e in range(2)], 1)
                 w2b[slot * 64 : (slot + 1) * 64, j * 256 + t * 128 : j * 256 + (t + 1) * 128] = tile.astype(BF16)
-    sent.append(fetch(w2b, w2b_o))
 
     m, k = iota((256, 256), 0), iota((256, 256), 1)
     source = (m % 32) * 8 + ((m // 32) % 2) * 4 + m // 64
@@ -173,36 +170,18 @@
                 cot_f[q * 256 + s * 32 : q * 256 + (s + 1) * 32, n * 128 : (n + 1) * 128] = got[n * 32 : (n + 1) * 32, :]
         part = pl.ds(q * 256, 256)
         back2[part, :] = dot_n(cot_f[part, :], wide[...]) * tissue[0, q].astype(F32)
-        sent.append(fetch(cot_f.at[part], cot_o.at[part]))
-        sent.append(fetch(back2.at[part], back2_o.at[part]))
-    for copy in sent:
-        copy.wait()
 
 
 def main_kernel(
-    tissue, own_i, first_i, second_i, w1_i, w2_i, back2_i, w2b_i, cot_i, out_o, totals,
-    own, before, after, w1, w2, back2, w2b, cot_f,
+    tissue, own, first, second, w1, w2, back2, w2b, cot_f, out_o, totals,
     lines, cols, z, act, slope1, act_sh, act2, grad2, wide, mixed, out, sems,
 ):
     fetch = fetcher(sems)
     even = is_even()
 
-    @pl.when(even)
-    def _():
-        pltpu.make_async_copy(second_i, before, sems.at[8]).start()
-        pltpu.make_async_copy(first_i, after, sems.at[9]).start()
-
-    @pl.when(jnp.logical_not(even))
-    def _():
-        pltpu.make_async_copy(first_i, before, sems.at[8]).start()
-        pltpu.make_async_copy(second_i, after, sems.at[9]).start()
-
-    in_image = [fetch(own_i, own)]
-    in_image += [pltpu.make_async_copy(first_i, before, sems.at[8]), pltpu.make_async_copy(second_i, after, sems.at[9])]
-    in_w1 = fetch(w1_i, w1)
-    in_w2 = fetch(w2_i, w2)
-    in_back = [fetch(back2_i, back2), fetch(w2b_i, w2b)]
-    in_cot = fetch(cot_i, cot_f)
+    def received(rows, lanes):
+        a, b = first[rows, lanes].astype(F32), second[rows, lanes].astype(F32)
+        return jnp.where(even, b, a), jnp.where(even, a, b)
 
     m, x = iota((128, 512), 0), iota((128, 512), 1)
     pick = (x == jnp.where(x < 256, 2 * m, 2 * m + 257)).astype(F32).astype(BF16)
@@ -214,12 +193,11 @@
     wide[PAD + 1024 :, :] = jnp.zeros((PAD, 768), F32)
     lines[63:64, :] = jnp.zeros((1, 2048), F32)
     none = jnp.zeros((64, 256), BF16)
-    for copy in in_image:
-        copy.wait()
     for k in range(3):
-        lines[21 * k : 21 * k + 7, :] = before[32 + 8 * k : 40 + 8 * k, :].astype(F32)[1:8]
+        before, after = received(slice(32 + 8 * k, 40 + 8 * k), slice(None))
+        lines[21 * k : 21 * k + 7, :] = before[1:8]
         lines[21 * k + 7 : 21 * k + 15, :] = own[0, k].astype(F32)
-        lines[21 * k + 15 : 21 * k + 21, :] = after[32 + 8 * k : 40 + 8 * k, :].astype(F32)[0:6]
+        lines[21 * k + 15 : 21 * k + 21, :] = after[0:6]
     for t in range(8):
         part = lines[:, t * 256 : (t + 1) * 256].astype(BF16)
         spread = jnp.concatenate([jnp.concatenate([part, none], 0), jnp.concatenate([none, part], 0)], 1)
@@ -227,7 +205,6 @@
 
     position = lax.axis_index("tile")
     ends = jnp.where(lane_is_low(1), (position > 0).astype(F32), (position < lax.axis_size("tile") - 1).astype(F32))
-    in_w1.wait()
     for t in range(CHUNKS):
         at = t * WIDE
         wins = [cols[PAD + at + s : PAD + at + s + WIDE, :].astype(BF16) for s in (-2, -1, 0, 1)]
@@ -242,9 +219,6 @@
         slope1[at : at + WIDE, :] = (sig * (1.0 + pre * (1.0 - sig)))[:, :256]
 
     low = lane_is_low(128)
-    in_w2.wait()
-    for copy in in_back:
-        copy.wait()
     for t in range(1024 // SPAN):
         at = t * SPAN
         wins = [act[PAD + at + j - 1 : PAD + at + j - 1 + SPAN, :].astype(BF16) for j in range(3)]
@@ -259,8 +233,8 @@
         sig = sigmoid(pre)
         ends = []
         for u in range(at // 128, (at + SPAN) // 128):
-            tiles = [(u // 2) * 4 + v for v in range(4)]
-            a, b = (jnp.concatenate([ref[0:32, v * 128 : (v + 1) * 128] for v in tiles], 0).astype(F32) for ref in (before, after))
+            tiles = [received(slice(0, 32), slice(v * 128, (v + 1) * 128)) for v in range((u // 2) * 4, (u // 2) * 4 + 4)]
+            a, b = (jnp.concatenate(half, 0) for half in zip(*tiles))
             ends.append(jnp.where(low, turn(a), b) if u % 2 else jnp.where(low, a, turn(b)))
         slope = sig * (1.0 + pre * (1.0 - sig))
         grad2[at : at + SPAN, 256:384] = (jnp.concatenate(ends, 0) * slope).astype(BF16)
@@ -312,7 +286,6 @@
             a, b = halves[2 * u + 1]
             totals[u * 64 : (u + 1) * 64, :] = jnp.where(low, left, turn(a) + b)
 
-    in_cot.wait()
     total = None
     for t in range(2):
         both = dot_0(act2[:, t * 128 : (t + 1) * 128], cot_f[:, t * 512 : (t + 1) * 512])
@@ -358,6 +331,14 @@
     return [jax.ShapeDtypeStruct(shape, dtype) for shape, dtype in pairs]
 
 
+def near(value):
+    return pltpu.with_memory_space_constraint(value, pltpu.VMEM)
+
+
+def far(value):
+    return pltpu.with_memory_space_constraint(value, pltpu.HBM)
+
+
 SMEM = pl.BlockSpec(memory_space=pltpu.SMEM)
 WHOLE = pl.BlockSpec(memory_space=pltpu.VMEM)
 APART = pl.BlockSpec(memory_space=pl.ANY)
@@ -368,43 +349,44 @@
     return pl.pallas_call(
         prepare_kernel,
         in_specs=[SMEM, APART, WHOLE, WHOLE, WHOLE],
-        out_specs=[APART] * 5,
-        out_shape=shapes(*outs),
-        scratch_shapes=[pltpu.VMEM((8192, 128), BF16)]
-        + [pltpu.VMEM(shape, dtype) for shape, dtype in outs]
-        + [pltpu.VMEM((1024, 256), BF16), pltpu.VMEM((128, 640), F32), pltpu.SemaphoreType.DMA((15,))],
+        out_specs=[WHOLE] * 5,
+        out_shape=[pltpu.VMEM(shape, dtype) for shape, dtype in outs],
+        scratch_shapes=[
+            pltpu.VMEM((8192, 128), BF16),
+            pltpu.VMEM((1024, 256), BF16),
+            pltpu.VMEM((128, 640), F32),
+            pltpu.SemaphoreType.DMA((4,)),
+        ],
         compiler_params=params(),
         name="prepare",
-    )(tissue, cot, expand, stem_t, conv_t)
+    )(far(tissue), far(cot), expand, stem_t, conv_t)
 
 
 def edges(tissue, cot, image, expand):
     return pl.pallas_call(
         edges_kernel,
-        in_specs=[SMEM, APART, WHOLE, WHOLE],
+        in_specs=[SMEM, APART, APART, APART],
         out_specs=[WHOLE] * 2,
-        out_shape=shapes(((56, 2048), BF16), ((56, 2048), BF16)),
-        scratch_shapes=[pltpu.VMEM((8192, 128), BF16), pltpu.VMEM((1024, 512), BF16), pltpu.SemaphoreType.DMA((4,))],
+        out_shape=[pltpu.VMEM((56, 2048), BF16)] * 2,
+        scratch_shapes=[
+            pltpu.VMEM((8192, 128), BF16),
+            pltpu.VMEM((1, 3, 8, 2048), BF16),
+            pltpu.VMEM((64, 256), BF16),
+            pltpu.VMEM((1024, 512), BF16),
+            pltpu.SemaphoreType.DMA((6,)),
+        ],
         compiler_params=params(),
         name="edges",
-    )(tissue, cot, image, expand)
-
-
-def main(tissue, own, first, second, w1, w2, back2, w2b, cot_f):
+    )(far(tissue), far(cot), far(image), far(expand))
+
+
+def main(tissue, *others):
     return pl.pallas_call(
         main_kernel,
-        in_specs=[SMEM] + [APART] * 8,
+        in_specs=[SMEM] + [WHOLE] * 8,
         out_specs=[APART, WHOLE],
-        out_shape=shapes(((2048, 128), BF16), ((512, 128), F32)),
+        out_shape=[jax.ShapeDtypeStruct((2048, 128), BF16), pltpu.VMEM((512, 128), F32)],
         scratch_shapes=[
-            pltpu.VMEM((1, 3, 8, 2048), BF16),
-            pltpu.VMEM((56, 2048), BF16),
-            pltpu.VMEM((56, 2048), BF16),
-            pltpu.VMEM((512, 512), BF16),
-            pltpu.VMEM((1536, 384), BF16),
-            pltpu.VMEM((1024, 256), F32),
-            pltpu.VMEM((384, 768), BF16),
-            pltpu.VMEM((1024, 1024), BF16),
             pltpu.VMEM((64, 2048), F32),
             pltpu.VMEM((1024 + 2 * PAD, 128), F32),
             pltpu.VMEM((1024, 512), BF16),
@@ -416,11 +398,11 @@
             pltpu.VMEM((1024 + 2 * PAD, 768), F32),
             pltpu.VMEM((2, 1024, 256), BF16),
             pltpu.VMEM((2048, 128), BF16),
-            pltpu.SemaphoreType.DMA((10,)),
+            pltpu.SemaphoreType.DMA((2,)),
         ],
         compiler_params=params(),
         name="main",
-    )(tissue, own, first, second, w1, w2, back2, w2b, cot_f)
+    )(far(tissue), *map(near, others))
 
 
 def unpack(totals):
@@ -431,7 +413,7 @@
         out_shape=shapes(((64, 147), F32), ((64, 576), F32), ((64, 256), F32)),
         compiler_params=params(),
         name="unpack",
-    )(totals)
+    )(near(totals))
 
 
 def reduce_all(totals):

time: 77.1 us -> 71.4 us (0.926)
  Pallas kernels: 23.1 us -> 18.5 us
    pallas_call x2, Pallas kernels: 15.3 us -> 11.8 us  [the longest x1 7.83 us: main(): pl.pallas_call(main_kernel, in_specs=[SMEM] + [WHOLE] * 8, out_specs=[APA...]
    pallas_call x1, Pallas kernels: 1.67 us -> 0.72 us  [unpack(): pl.pallas_call(unpack_kernel, in_specs=[WHOLE], out_specs=[WHOLE] * 3, ou...]
where the time goes in v3:
time: 71.4 us; the launch traced here: 71.1 us
  blocking collectives  48.5 us (68%)
  Pallas kernels  18.5 us (26%)
  starting transfers between devices  3.22 us (5%)
  between operations  0.77 us (1%)
    all_to_all x1, blocking collectives, reduce_all(): lax.all_to_all(jnp.broadcast_to(part[None], (depth,) + part.shape), 'tile...  17.8 us
    all_to_all x1, blocking collectives, reduce_all(): lax.all_to_all(totals.reshape(count, -1, 128), slide, 0, 0, tiled=True)  16.8 us
    all_to_all x1, blocking collectives, reduce_all(): lax.all_to_all(jnp.broadcast_to(part[None], (count,) + part.shape), slide...  13.9 us
    pallas_call x1, Pallas kernels, main(): pl.pallas_call(main_kernel, in_specs=[SMEM] + [WHOLE] * 8, out_specs=[APA...  7.83 us
    pallas_call x1, Pallas kernels, prepare(): pl.pallas_call(prepare_kernel, in_specs=[SMEM, APART, WHOLE, WHOLE, WHOLE...  5.9 us
    pallas_call x1, Pallas kernels, edges(): pl.pallas_call(edges_kernel, in_specs=[SMEM, APART, APART, APART], out_sp...  4.02 us
    ppermute x1, starting transfers between devices, per_device(): lax.ppermute(first, 'tile', pairs[0] + [(b, a) for a, b in pairs[0]])  2.55 us
  transfers between devices with their start and end apart: 2, of which 0 were waited for; matrix products, arithmetic and copies ran while one was open for 0% of the time, Pallas kernels for 8%

profile of v3, /device:TPU:1, one launch (start us, length us, event | category | flops | bytes accessed | tf_op | source)
XLA Modules:
  0.0 71.1 jit_solution(7647391055305630108)
XLA Ops:
  0.6 0.0 copy-start.1
  0.6 0.0 copy-start.2
  0.7 0.0 copy-start.3
  0.7 0.0 copy-start
  0.7 4.0 %edges.1 = (bf16[56,2048]{1,0:T(8,128)(2,1)S(1)}, bf16[56,2048]{1,0:T(8,128)(2,1)S(1)}) custom-call(s32[1,4]{1,0:T(1,128)} %bitcast.23, bf16[8192,128]{1,0:T(8,128)(2,1)} %bitcast.21, bf16[1,3,8,2048]{3,2,1,0:T(8,128)(2,1)} %own.1, bf16[64,256]{1,0:T(8,128)(2,1)} %expand.1), custom_call_target="tpu_custom_call" | custom-call | tf_op jit(solution)/shard_map/edges/pallas_call | solution.py:366
  4.7 2.6 %collective-permute-start = (bf16[56,2048]{1,0:T(8,128)(2,1)S(1)}, bf16[56,2048]{1,0:T(8,128)(2,1)S(1)}, u32[]{:S(2)}, u32[]{:S(2)}) collective-permute-start(bf16[56,2048]{1,0:T(8,128)(2,1)S(1)} %get-tuple-element.16), channel_id=1, source_target_pairs={{0,1},{2,3},{4,5},{6,7},{1,0},{3,2},{5,4},{7,6},{8,9},{10,11},{12,... | collective-permute-start | bytes 688136 | tf_op jit(solution)/shard_map/ppermute | solution.py:434
  7.3 0.7 collective-permute-start.1
  7.9 0.0 copy-done.1
  7.9 0.0 copy-done.2
  7.9 0.0 copy-done.3
  8.0 5.9 %prepare.1 = (bf16[1024,1024]{1,0:T(8,128)(2,1)S(1)}, f32[1024,256]{1,0:T(8,128)S(1)}, bf16[512,512]{1,0:T(8,128)(2,1)S(1)}, bf16[1536,384]{1,0:T(8,128)(2,1)S(1)}, bf16[384,768]{1,0:T(8,128)(2,1)S(1)}) custom-call(s32[1,4]{1,0:T(1,128)} %bitcast.24, bf16[8192,128]{1,0:T(8,128)(2,1)} %bitcast.22, bf16[64,256]{1,0:T(8,128)(2,1)S(1)} %copy-done.1, ...), custom_call_target="tpu_custom_call" | custom-call | tf_op jit(solution)/shard_map/prepare/pallas_call | solution.py:349
  13.9 0.0 collective-permute-done.first
  13.9 0.0 collective-permute-done.1.second
  13.9 0.0 copy-done
  13.9 7.8 %main.1 = (bf16[2048,128]{1,0:T(8,128)(2,1)}, f32[512,128]{1,0:T(8,128)S(1)}) custom-call(s32[1,4]{1,0:T(1,128)} %bitcast.25, bf16[1,3,8,2048]{3,2,1,0:T(8,128)(2,1)S(1)} %copy-done, bf16[56,2048]{1,0:T(8,128)(2,1)S(1)} %collective-permute-done.first, bf16[56,2048]{1,0:T(8,128)(2,1)S(1)} %collective-permute-done.1.second, ...), custom_call_target="tpu_custom_call" | custom-call | tf_op jit(solution)/shard_map/main/pallas_call | solution.py:384
  21.7 16.8 %all_to_all.15 = f32[32,16,128]{2,1,0:T(8,128)S(1)} all-to-all(f32[32,16,128]{2,1,0:T(8,128)S(1)} %bitcast.18), channel_id=1, replica_groups=mesh['x'=4,'y'=4,'core'=2,'tile'=8] {'x','y','core'}, dimensions={0} | all-to-all | bytes 524288 | tf_op jit(solution)/shard_map/all_to_all | solution.py:422
  38.6 17.8 %all_to_all.16 = f32[8,16,128]{2,1,0:T(8,128)S(1)} all-to-all(f32[8,16,128]{2,1,0:T(8,128)S(1)} %broadcast_in_dim.4), channel_id=1, replica_groups=mesh['x'=4,'y'=4,'core'=2,'tile'=8] {'tile'}, dimensions={0} | all-to-all | bytes 131072 | tf_op jit(solution)/shard_map/all_to_all | solution.py:423
  56.4 13.9 %all_to_all.17 = f32[32,16,128]{2,1,0:T(8,128)S(1)} all-to-all(f32[32,16,128]{2,1,0:T(8,128)S(1)} %broadcast_in_dim.5), channel_id=1, replica_groups=mesh['x'=4,'y'=4,'core'=2,'tile'=8] {'x','y','core'}, dimensions={0} | all-to-all | bytes 524288 | tf_op jit(solution)/shard_map/all_to_all | solution.py:424
  70.4 0.7 %unpack.1 = (f32[64,147]{1,0:T(8,128)}, f32[64,576]{1,0:T(8,128)}, f32[64,256]{1,0:T(8,128)}) custom-call(f32[512,128]{1,0:T(8,128)S(1)} %bitcast.17), custom_call_target="tpu_custom_call" | custom-call | tf_op jit(solution)/shard_map/unpack/pallas_call | solution.py:409
  (4 shorter events, 0.1 us)
Async XLA Ops:
  0.6 7.3 %copy-start.1 = (bf16[64,256]{1,0:T(8,128)(2,1)S(1)}, bf16[64,256]{1,0:T(8,128)(2,1)}, u32[]{:S(2)}) copy-start(bf16[64,256]{1,0:T(8,128)(2,1)} %expand.1) | copy-start | bytes 98308
  0.6 7.3 %copy-start.2 = (bf16[576,64]{0,1:T(8,128)(2,1)S(1)}, bf16[576,64]{0,1:T(8,128)(2,1)}, u32[]{:S(2)}) copy-start(bf16[576,64]{0,1:T(8,128)(2,1)} %param.8) | copy-start | bytes 221188
  0.7 7.3 %copy-start.3 = (bf16[147,64]{0,1:T(8,128)(2,1)S(1)}, bf16[147,64]{0,1:T(8,128)(2,1)}, u32[]{:S(2)}) copy-start(bf16[147,64]{0,1:T(8,128)(2,1)} %param.7) | copy-start | bytes 56452
  0.7 13.2 %copy-start = (bf16[1,3,8,2048]{3,2,1,0:T(8,128)(2,1)S(1)}, bf16[1,3,8,2048]{3,2,1,0:T(8,128)(2,1)}, u32[]{:S(2)}) copy-start(bf16[1,3,8,2048]{3,2,1,0:T(8,128)(2,1)} %own.1) | copy-start | bytes 294916
  4.7 9.2 %collective-permute-start = (bf16[56,2048]{1,0:T(8,128)(2,1)S(1)}, bf16[56,2048]{1,0:T(8,128)(2,1)S(1)}, u32[]{:S(2)}, u32[]{:S(2)}) collective-permute-start(bf16[56,2048]{1,0:T(8,128)(2,1)S(1)} %get-tuple-element.16), channel_id=1, source_target_pairs={{0,1},{2,3},{4,5},{6,7},{1,0},{3,2},{5,4},{7,6},{8,9},{10,11},{12,... | collective-permute-start | bytes 688136 | tf_op jit(solution)/shard_map/ppermute | solution.py:434
  7.3 6.6 %collective-permute-start.1 = (bf16[56,2048]{1,0:T(8,128)(2,1)S(1)}, bf16[56,2048]{1,0:T(8,128)(2,1)S(1)}, u32[]{:S(2)}, u32[]{:S(2)}) collective-permute-start(bf16[56,2048]{1,0:T(8,128)(2,1)S(1)} %get-tuple-element.17), channel_id=1, source_target_pairs={{1,2},{3,4},{5,6},{2,1},{4,3},{6,5},{9,10},{11,12},{13,14},{10,9},... | collective-permute-start | bytes 688136 | tf_op jit(solution)/shard_map/ppermute | solution.py:435

commit v4 on v3

--- a/solution.py
+++ b/solution.py
@@ -89,8 +89,9 @@
     low = lane_is_low(256)
     wide = jnp.concatenate([jnp.where(low, both, 0.0), jnp.where(low, 0.0, both)], 0).astype(BF16)
     low = lane_is_low(128)
+    for part in parts:
+        part.wait()
     for q in range(4):
-        parts[q].wait()
         for s in range(8):
             got = dot_n(order, cot[q * 2048 + s * 256 : q * 2048 + (s + 1) * 256, :]).astype(BF16)
             for n in range(4):
@@ -314,13 +315,13 @@
 
 def unpack_kernel(totals, stem_t, conv_t, expand):
     for u in range(4):
-        conv_t[:, u * 128 : (u + 1) * 128] = totals[u * 64 : (u + 1) * 64, :]
-    mixed = totals[256:320, :]
+        conv_t[:, u * 128 : (u + 1) * 128] = totals[u * 64 : (u + 1) * 64, :].astype(F32)
+    mixed = totals[256:320, :].astype(F32)
     conv_t[:, 512:576] = mixed[:, 0:64]
-    stem_t[:, 0:128] = totals[448:512, :]
+    stem_t[:, 0:128] = totals[448:512, :].astype(F32)
     stem_t[:, 128:147] = turn(mixed)[:, 0:19]
     for u in range(2):
-        expand[:, u * 128 : (u + 1) * 128] = totals[320 + u * 64 : 384 + u * 64, :]
+        expand[:, u * 128 : (u + 1) * 128] = totals[320 + u * 64 : 384 + u * 64, :].astype(F32)
 
 
 def params():
@@ -421,6 +422,7 @@
     count, depth = lax.axis_size(slide), lax.axis_size("tile")
     part = lax.all_to_all(totals.reshape(count, -1, 128), slide, 0, 0, tiled=True).sum(0)
     part = lax.all_to_all(jnp.broadcast_to(part[None], (depth,) + part.shape), "tile", 0, 0, tiled=True).sum(0)
+    part = part.astype(BF16)
     whole = lax.all_to_all(jnp.broadcast_to(part[None], (count,) + part.shape), slide, 0, 0, tiled=True)
     return whole.reshape(totals.shape)
 

time: 71.4 us -> 69.9 us (0.979)
  blocking collectives: 48.5 us -> 47.3 us
    all_to_all x1, blocking collectives: 13.9 us -> 12.7 us  [reduce_all(): lax.all_to_all(jnp.broadcast_to(part[None], (count,) + part.shape), slide...]
where the time goes in v4:
time: 69.9 us; the launch traced here: 69.6 us
  blocking collectives  47.3 us (68%)
  Pallas kernels  18.3 us (26%)
  starting transfers between devices  3.21 us (5%)
  between operations  0.77 us (1%)
    all_to_all x1, blocking collectives, reduce_all(): lax.all_to_all(jnp.broadcast_to(part[None], (depth,) + part.shape), 'tile...  17.8 us
    all_to_all x1, blocking collectives, reduce_all(): lax.all_to_all(totals.reshape(count, -1, 128), slide, 0, 0, tiled=True)  16.8 us
    all_to_all x1, blocking collectives, reduce_all(): lax.all_to_all(jnp.broadcast_to(part[None], (count,) + part.shape), slide...  12.7 us
    pallas_call x1, Pallas kernels, main(): pl.pallas_call(main_kernel, in_specs=[SMEM] + [WHOLE] * 8, out_specs=[APA...  7.83 us
    pallas_call x1, Pallas kernels, prepare(): pl.pallas_call(prepare_kernel, in_specs=[SMEM, APART, WHOLE, WHOLE, WHOLE...  5.9 us
    pallas_call x1, Pallas kernels, edges(): pl.pallas_call(edges_kernel, in_specs=[SMEM, APART, APART, APART], out_sp...  3.83 us
    ppermute x1, starting transfers between devices, per_device(): lax.ppermute(first, 'tile', pairs[0] + [(b, a) for a, b in pairs[0]])  2.55 us
  transfers between devices with their start and end apart: 2, of which 0 were waited for; matrix products, arithmetic and copies ran while one was open for 0% of the time, Pallas kernels for 8%

profile of v4, /device:TPU:1, one launch (start us, length us, event | category | flops | bytes accessed | tf_op | source)
XLA Modules:
  0.0 69.6 jit_solution(12802440312320769505)
XLA Ops:
  0.6 0.0 copy-start.1
  0.6 0.0 copy-start.2
  0.7 0.0 copy-start.3
  0.7 0.0 copy-start
  0.7 3.8 %edges.1 = (bf16[56,2048]{1,0:T(8,128)(2,1)S(1)}, bf16[56,2048]{1,0:T(8,128)(2,1)S(1)}) custom-call(s32[1,4]{1,0:T(1,128)} %bitcast.23, bf16[8192,128]{1,0:T(8,128)(2,1)} %bitcast.21, bf16[1,3,8,2048]{3,2,1,0:T(8,128)(2,1)} %own.1, bf16[64,256]{1,0:T(8,128)(2,1)} %expand.1), custom_call_target="tpu_custom_call" | custom-call | tf_op jit(solution)/shard_map/edges/pallas_call | solution.py:367
  4.5 2.5 %collective-permute-start = (bf16[56,2048]{1,0:T(8,128)(2,1)S(1)}, bf16[56,2048]{1,0:T(8,128)(2,1)S(1)}, u32[]{:S(2)}, u32[]{:S(2)}) collective-permute-start(bf16[56,2048]{1,0:T(8,128)(2,1)S(1)} %get-tuple-element.16), channel_id=1, source_target_pairs={{0,1},{2,3},{4,5},{6,7},{1,0},{3,2},{5,4},{7,6},{8,9},{10,11},{12,... | collective-permute-start | bytes 688136 | tf_op jit(solution)/shard_map/ppermute | solution.py:436
  7.1 0.7 collective-permute-start.1
  7.7 0.0 copy-done.1
  7.7 0.0 copy-done.2
  7.7 0.0 copy-done.3
  7.8 5.9 %prepare.1 = (bf16[1024,1024]{1,0:T(8,128)(2,1)S(1)}, f32[1024,256]{1,0:T(8,128)S(1)}, bf16[512,512]{1,0:T(8,128)(2,1)S(1)}, bf16[1536,384]{1,0:T(8,128)(2,1)S(1)}, bf16[384,768]{1,0:T(8,128)(2,1)S(1)}) custom-call(s32[1,4]{1,0:T(1,128)} %bitcast.24, bf16[8192,128]{1,0:T(8,128)(2,1)} %bitcast.22, bf16[64,256]{1,0:T(8,128)(2,1)S(1)} %copy-done.1, ...), custom_call_target="tpu_custom_call" | custom-call | tf_op jit(solution)/shard_map/prepare/pallas_call | solution.py:350
  13.7 0.0 collective-permute-done.first
  13.7 0.0 collective-permute-done.1.second
  13.7 0.0 copy-done
  13.7 7.8 %main.1 = (bf16[2048,128]{1,0:T(8,128)(2,1)}, f32[512,128]{1,0:T(8,128)S(1)}) custom-call(s32[1,4]{1,0:T(1,128)} %bitcast.25, bf16[1,3,8,2048]{3,2,1,0:T(8,128)(2,1)S(1)} %copy-done, bf16[56,2048]{1,0:T(8,128)(2,1)S(1)} %collective-permute-done.first, bf16[56,2048]{1,0:T(8,128)(2,1)S(1)} %collective-permute-done.1.second, ...), custom_call_target="tpu_custom_call" | custom-call | tf_op jit(solution)/shard_map/main/pallas_call | solution.py:385
  21.5 16.8 %all_to_all.15 = f32[32,16,128]{2,1,0:T(8,128)S(1)} all-to-all(f32[32,16,128]{2,1,0:T(8,128)S(1)} %bitcast.18), channel_id=1, replica_groups=mesh['x'=4,'y'=4,'core'=2,'tile'=8] {'x','y','core'}, dimensions={0} | all-to-all | bytes 524288 | tf_op jit(solution)/shard_map/all_to_all | solution.py:423
  38.4 17.8 %all_to_all.16 = f32[8,16,128]{2,1,0:T(8,128)S(1)} all-to-all(f32[8,16,128]{2,1,0:T(8,128)S(1)} %broadcast_in_dim.4), channel_id=1, replica_groups=mesh['x'=4,'y'=4,'core'=2,'tile'=8] {'tile'}, dimensions={0} | all-to-all | bytes 131072 | tf_op jit(solution)/shard_map/all_to_all | solution.py:424
  56.2 12.7 %all_to_all.17 = bf16[32,16,128]{2,1,0:T(8,128)(2,1)S(1)} all-to-all(bf16[32,16,128]{2,1,0:T(8,128)(2,1)S(1)} %broadcast_in_dim.5), channel_id=1, replica_groups=mesh['x'=4,'y'=4,'core'=2,'tile'=8] {'x','y','core'}, dimensions={0} | all-to-all | bytes 262144 | tf_op jit(solution)/shard_map/all_to_all | solution.py:426
  68.9 0.7 %unpack.1 = (f32[64,147]{1,0:T(8,128)}, f32[64,576]{1,0:T(8,128)}, f32[64,256]{1,0:T(8,128)}) custom-call(bf16[512,128]{1,0:T(8,128)(2,1)S(1)} %bitcast.17), custom_call_target="tpu_custom_call" | custom-call | tf_op jit(solution)/shard_map/unpack/pallas_call | solution.py:410
  (4 shorter events, 0.1 us)
Async XLA Ops:
  0.6 7.1 %copy-start.1 = (bf16[64,256]{1,0:T(8,128)(2,1)S(1)}, bf16[64,256]{1,0:T(8,128)(2,1)}, u32[]{:S(2)}) copy-start(bf16[64,256]{1,0:T(8,128)(2,1)} %expand.1) | copy-start | bytes 98308
  0.6 7.1 %copy-start.2 = (bf16[576,64]{0,1:T(8,128)(2,1)S(1)}, bf16[576,64]{0,1:T(8,128)(2,1)}, u32[]{:S(2)}) copy-start(bf16[576,64]{0,1:T(8,128)(2,1)} %param.8) | copy-start | bytes 221188
  0.7 7.1 %copy-start.3 = (bf16[147,64]{0,1:T(8,128)(2,1)S(1)}, bf16[147,64]{0,1:T(8,128)(2,1)}, u32[]{:S(2)}) copy-start(bf16[147,64]{0,1:T(8,128)(2,1)} %param.7) | copy-start | bytes 56452
  0.7 13.0 %copy-start = (bf16[1,3,8,2048]{3,2,1,0:T(8,128)(2,1)S(1)}, bf16[1,3,8,2048]{3,2,1,0:T(8,128)(2,1)}, u32[]{:S(2)}) copy-start(bf16[1,3,8,2048]{3,2,1,0:T(8,128)(2,1)} %own.1) | copy-start | bytes 294916
  4.5 9.2 %collective-permute-start = (bf16[56,2048]{1,0:T(8,128)(2,1)S(1)}, bf16[56,2048]{1,0:T(8,128)(2,1)S(1)}, u32[]{:S(2)}, u32[]{:S(2)}) collective-permute-start(bf16[56,2048]{1,0:T(8,128)(2,1)S(1)} %get-tuple-element.16), channel_id=1, source_target_pairs={{0,1},{2,3},{4,5},{6,7},{1,0},{3,2},{5,4},{7,6},{8,9},{10,11},{12,... | collective-permute-start | bytes 688136 | tf_op jit(solution)/shard_map/ppermute | solution.py:436
  7.1 6.6 %collective-permute-start.1 = (bf16[56,2048]{1,0:T(8,128)(2,1)S(1)}, bf16[56,2048]{1,0:T(8,128)(2,1)S(1)}, u32[]{:S(2)}, u32[]{:S(2)}) collective-permute-start(bf16[56,2048]{1,0:T(8,128)(2,1)S(1)} %get-tuple-element.17), channel_id=1, source_target_pairs={{1,2},{3,4},{5,6},{2,1},{4,3},{6,5},{9,10},{11,12},{13,14},{10,9},... | collective-permute-start | bytes 688136 | tf_op jit(solution)/shard_map/ppermute | solution.py:437
